TPU v7x, 256 devices: a whole 4x4x8 slice. The times are simulated.
256 devices in a mesh: dp: 64 (over x, z, core), sub: 4 (over y).
Axes of the slice: x: 4, y: 4, z: 8, core: 2. Of those that a mesh axis runs over, the one named last changes fastest.
Arguments:
- tokens: bfloat16 [32768, 512], P('dp', 'sub'), may hold values from -6 to 6
- lengths: int32 [128], replicated, may hold values from 1 to 512, 32768 in all
- weight_in: bfloat16 [512, 2048], P(None, 'sub'), may hold values from -0.25 to 0.25
- weight_out: bfloat16 [512, 512], P('sub'), may hold values from -0.25 to 0.25
- grad_out: bfloat16 [32768, 512], P('dp', 'sub'), may hold values from -6 to 6
Outputs:
- layer_output: bfloat16 [32768, 512], P('dp', 'sub')
- grad_tokens: bfloat16 [32768, 512], P('dp', 'sub')
- grad_win: float32 [512, 2048], P(None, 'sub')
- grad_wout: float32 [512, 512], P('sub')
Inputs may be any that keep to these rules, and one draw needn't show every extreme that they name: The 128 lengths sum to 32768; histories lie end to end in order, so one may begin on one index of dp and end on the next; the longest is exactly 512.
All inputs are finite; a program needn't handle non-finite values.
Results may differ from a plain program's by a relative error of at most 0.0076.
Values may be sent and summed in bfloat16 or wider, within the bound.
A program may use at most 64 MiB of HBM per device.

v0:
```python
import math

import jax
import jax.numpy as jnp
from jax import lax
from jax.sharding import PartitionSpec as P

EPSILON = 1e-05


def shifted(value, axis, by):
    length = lax.axis_size(axis)
    pairs = [(i, i + by) for i in range(length) if 0 <= i + by < length]
    return lax.ppermute(value, axis, pairs)


def contract_rows(left_op, right_op):
    return lax.dot_general(
        left_op, right_op, (((0,), (0,)), ((), ())), preferred_element_type=jnp.float32
    )


def contract_cols(left_op, right_op):
    return lax.dot_general(
        left_op, right_op, (((1,), (1,)), ((), ())), preferred_element_type=jnp.float32
    )


def norm_rows(values):
    row_mean = jnp.mean(values, axis=1, keepdims=True)
    centred = values - row_mean
    inv_std = lax.rsqrt(jnp.mean(centred * centred, axis=1, keepdims=True) + EPSILON)
    return (centred * inv_std, inv_std)


def silu_slope(values):
    sigmoid = jax.nn.sigmoid(values)
    return sigmoid * (1.0 + values * (1.0 - sigmoid))


def boundary(starts, seq_ends, edge_row):
    inside = (starts < edge_row) & (seq_ends > edge_row)
    after_edge = jnp.sum(jnp.where(inside, seq_ends - edge_row, 0))
    before_edge = jnp.sum(jnp.where(inside, edge_row - starts, 0))
    return (after_edge, before_edge)


def seq_lookup(starts, global_rows):
    return jnp.sum((starts[None, :] <= global_rows[:, None]).astype(jnp.int32), 1) - 1


def tile_weights(q_rows, k_rows, q_ids, k_ids, q_first, k_first, tile_rows, head_dim):
    scores = contract_cols(q_rows, k_rows) / math.sqrt(head_dim)
    q_pos = q_first + jnp.arange(tile_rows)
    k_pos = k_first + jnp.arange(tile_rows)
    allowed = (q_ids[:, None] == k_ids[None, :]) & (k_pos[None, :] <= q_pos[:, None])
    return (scores, allowed)


def attend_forward(queries, key_rows, values, query_ids, key_ids, first_block, tile_rows):
    total_rows, head_dim = queries.shape
    tile_count = total_rows // tile_rows

    def per_query(query_block, output):
        q_first = query_block * tile_rows
        q_rows = lax.dynamic_slice_in_dim(queries, q_first, tile_rows, 0)
        q_ids = lax.dynamic_slice_in_dim(query_ids, q_first, tile_rows, 0)

        def per_key(k_index, summed):
            k_first = k_index * tile_rows
            k_rows = lax.dynamic_slice_in_dim(key_rows, k_first, tile_rows, 0)
            v_rows = lax.dynamic_slice_in_dim(values, k_first, tile_rows, 0)
            k_ids = lax.dynamic_slice_in_dim(key_ids, k_first, tile_rows, 0)
            scores, allowed = tile_weights(
                q_rows, k_rows, q_ids, k_ids, q_first, k_first, tile_rows, head_dim
            )
            weights = jnp.where(allowed, jax.nn.silu(scores), 0.0).astype(jnp.bfloat16)
            return summed + jnp.dot(weights, v_rows, preferred_element_type=jnp.float32)

        summed = lax.fori_loop(
            first_block[query_block],
            query_block + 1,
            per_key,
            jnp.zeros((tile_rows, head_dim), jnp.float32),
        )
        return lax.dynamic_update_slice_in_dim(output, summed, q_first, 0)

    return lax.fori_loop(0, tile_count, per_query, jnp.zeros((total_rows, head_dim), jnp.float32))


def attend_backward(
    queries, key_rows, values, grad_rows, query_ids, key_ids, first_block, tile_rows
):
    total_rows, head_dim = queries.shape
    tile_count = total_rows // tile_rows
    zeros_all = jnp.zeros((total_rows, head_dim), jnp.float32)

    def per_query(query_block, carried):
        grad_query, grad_keys, grad_values = carried
        q_first = query_block * tile_rows
        q_rows = lax.dynamic_slice_in_dim(queries, q_first, tile_rows, 0)
        q_ids = lax.dynamic_slice_in_dim(query_ids, q_first, tile_rows, 0)
        g_rows = lax.dynamic_slice_in_dim(grad_rows, q_first, tile_rows, 0)

        def per_key(k_index, partial_value):
            summed, grad_keys, grad_values = partial_value
            k_first = k_index * tile_rows
            k_rows = lax.dynamic_slice_in_dim(key_rows, k_first, tile_rows, 0)
            v_rows = lax.dynamic_slice_in_dim(values, k_first, tile_rows, 0)
            k_ids = lax.dynamic_slice_in_dim(key_ids, k_first, tile_rows, 0)
            scores, allowed = tile_weights(
                q_rows, k_rows, q_ids, k_ids, q_first, k_first, tile_rows, head_dim
            )
            weights = jnp.where(allowed, jax.nn.silu(scores), 0.0).astype(jnp.bfloat16)
            d_weight = contract_cols(g_rows, v_rows)
            d_score = (
                jnp.where(allowed, d_weight * silu_slope(scores), 0.0) / math.sqrt(head_dim)
            ).astype(jnp.bfloat16)
            summed = summed + jnp.dot(d_score, k_rows, preferred_element_type=jnp.float32)
            key_part = lax.dynamic_slice_in_dim(grad_keys, k_first, tile_rows, 0) + contract_rows(
                d_score, q_rows
            )
            grad_keys = lax.dynamic_update_slice_in_dim(grad_keys, key_part, k_first, 0)
            value_part = lax.dynamic_slice_in_dim(
                grad_values, k_first, tile_rows, 0
            ) + contract_rows(weights, g_rows)
            grad_values = lax.dynamic_update_slice_in_dim(grad_values, value_part, k_first, 0)
            return (summed, grad_keys, grad_values)

        zeros_block = jnp.zeros((tile_rows, head_dim), jnp.float32)
        summed, grad_keys, grad_values = lax.fori_loop(
            first_block[query_block],
            query_block + 1,
            per_key,
            (zeros_block, grad_keys, grad_values),
        )
        grad_query = lax.dynamic_update_slice_in_dim(grad_query, summed, q_first, 0)
        return (grad_query, grad_keys, grad_values)

    return lax.fori_loop(0, tile_count, per_query, (zeros_all, zeros_all, zeros_all))


def shards(tokens, lengths, weight_in, weight_out, grad_out):
    full_x, full_grad = (
        lax.all_gather(tokens, "sub", axis=1, tiled=True),
        lax.all_gather(grad_out, "sub", axis=1, tiled=True),
    )
    row_count, full_width = full_x.shape
    head_dim = weight_out.shape[0]
    tile_rows = min(512, row_count)
    my_index = lax.axis_index("dp")
    first_row = my_index * row_count
    scaling = 1.0 / math.sqrt(row_count * lax.axis_size("dp"))
    x_hat, x_scale = norm_rows(full_x.astype(jnp.float32))
    x_normed = x_hat.astype(jnp.bfloat16)
    hidden = jnp.dot(x_normed, weight_in, preferred_element_type=jnp.float32)
    projected = lax.optimization_barrier(jax.nn.silu(hidden).astype(jnp.bfloat16))
    gate_u = projected[:, :head_dim].astype(jnp.float32)
    values = projected[:, head_dim : 2 * head_dim]
    queries = projected[:, 2 * head_dim : 3 * head_dim]
    key_rows = projected[:, 3 * head_dim :]
    seq_ends = jnp.cumsum(lengths)
    starts = seq_ends - lengths
    head_low, tail_low = boundary(starts, seq_ends, first_row)
    head_high, tail_high = boundary(starts, seq_ends, first_row + row_count)
    row_index = jnp.arange(row_count)
    own_global = first_row + row_index
    own_low = jnp.zeros((), jnp.bool_)
    own_high = jnp.ones((), jnp.bool_)
    from_below = (row_index < head_low) & jnp.logical_not(own_low)
    to_above = (row_index >= row_count - tail_high) & jnp.logical_not(own_high)
    own_valid = jnp.logical_not(from_below | to_above)
    upper_valid = own_high & (row_index < head_high)
    own_rows = (queries, key_rows, values)
    upper_rows = shifted((queries, key_rows, values), "dp", -1)
    sections = [own_rows, upper_rows]
    valids = [own_valid, upper_valid]
    placed = [own_global, own_global + row_count]
    offset = 0
    back_start = offset + row_count
    part_start = back_start + row_count
    buffer_q = jnp.concatenate([section[0] for section in sections], 0)
    buffer_k = jnp.concatenate([section[1] for section in sections], 0)
    buffer_v = jnp.concatenate([section[2] for section in sections], 0)
    live_rows = jnp.concatenate(valids, 0)
    global_row = jnp.concatenate(placed, 0)
    span_rows = live_rows.shape[0]
    seq_of_row = seq_lookup(starts, global_row)
    picked = jnp.arange(starts.shape[0])[None, :] == seq_of_row[:, None]
    seq_begin = jnp.sum(jnp.where(picked, starts[None, :], 0), 1)
    query_ids = jnp.where(live_rows, seq_of_row, -1)
    key_ids = jnp.where(live_rows, seq_of_row, -2)
    lowest = jnp.where(live_rows, jnp.arange(span_rows) - global_row + seq_begin, span_rows)
    first_block = jnp.min(lowest.reshape(span_rows // tile_rows, tile_rows), 1) // tile_rows
    attended = attend_forward(
        buffer_q, buffer_k, buffer_v, query_ids, key_ids, first_block, tile_rows
    )
    own_part = attended[offset:back_start]
    back_result = shifted(attended[back_start:part_start], "dp", 1)
    merged = jnp.where(from_below[:, None], back_result, own_part)
    row_total = lax.psum(jnp.sum(merged, 1), "sub")
    centred = merged - (row_total / full_width)[:, None]
    spread = lax.psum(jnp.sum(centred * centred, 1), "sub")
    inv_std = lax.rsqrt(spread / full_width + EPSILON)[:, None]
    normed = centred * inv_std
    gated_rows = (normed * gate_u).astype(jnp.bfloat16)
    layer_part = lax.psum_scatter(
        jnp.dot(gated_rows, weight_out, preferred_element_type=jnp.float32),
        "sub",
        scatter_dimension=1,
        tiled=True,
    )
    layer_output = (tokens.astype(jnp.float32) + layer_part).astype(jnp.bfloat16)
    d_gated = contract_cols(full_grad, weight_out)
    grad_wout = contract_rows(gated_rows, full_grad)
    d_normed = d_gated * gate_u
    d_gate = d_gated * normed
    sum_one, sum_two = lax.psum((jnp.sum(d_normed, 1), jnp.sum(d_normed * normed, 1)), "sub")
    d_attended = (
        inv_std
        * (d_normed - (sum_one / full_width)[:, None] - normed * (sum_two / full_width)[:, None])
    ).astype(jnp.bfloat16)
    upper_grad = shifted(d_attended, "dp", -1)
    grad_parts = [d_attended, upper_grad]
    grad_buffer = jnp.concatenate(grad_parts, 0)
    grad_query, grad_keys, grad_values = attend_backward(
        buffer_q, buffer_k, buffer_v, grad_buffer, query_ids, key_ids, first_block, tile_rows
    )
    back_q, back_k, back_v = shifted(
        (
            grad_query[back_start:part_start],
            grad_keys[back_start:part_start],
            grad_values[back_start:part_start],
        ),
        "dp",
        1,
    )
    mine_q = jnp.where(from_below[:, None], back_q, grad_query[offset:back_start])
    mine_k = jnp.where(from_below[:, None], back_k, grad_keys[offset:back_start])
    mine_v = jnp.where(from_below[:, None], back_v, grad_values[offset:back_start])
    d_hidden = (jnp.concatenate([d_gate, mine_v, mine_q, mine_k], 1) * silu_slope(hidden)).astype(
        jnp.bfloat16
    )
    grad_win = contract_rows(x_normed, d_hidden)
    d_input = contract_cols(d_hidden, weight_in)
    col_count = tokens.shape[1]
    sub_index = lax.axis_index("sub")
    summed_input = lax.psum(d_input, "sub")
    first_mean = jnp.mean(summed_input, axis=1, keepdims=True)
    second_mean = jnp.mean(summed_input * x_hat, axis=1, keepdims=True)
    d_full = x_scale * (summed_input - first_mean - x_hat * second_mean)
    d_piece = lax.dynamic_slice_in_dim(d_full, sub_index * col_count, col_count, 1)
    grad_tokens = (grad_out.astype(jnp.float32) + d_piece).astype(jnp.bfloat16)
    total_win, total_wout = lax.psum((grad_win, grad_wout), "dp")
    return (layer_output, grad_tokens, total_win * scaling, total_wout * scaling)


def solution(mesh):
    placed = (P("dp", "sub"), P(), P(None, "sub"), P("sub", None), P("dp", "sub"))
    return jax.shard_map(
        shards,
        mesh=mesh,
        in_specs=placed,
        out_specs=(P("dp", "sub"), P("dp", "sub"), P(None, "sub"), P("sub", None)),
        check_vma=False,
    )
```

profile of v0, /device:TPU:1, one launch (start us, length us, event | category | flops | bytes accessed | tf_op | source)
XLA Modules:
  0.0 439.4 jit_solution(15223046724128528377)
XLA Ops:
  7.2 14.1 %all_gather.6 = bf16[512,512]{1,0:T(8,128)(2,1)S(1)} all-gather(bf16[512,128]{1,0:T(8,128)(2,1)} %param.13), channel_id=1, replica_groups=mesh['dp'=64,'sub'=4] {'sub'}, dimensions={1}, use_global_device_ids=true | all-gather | bytes 655360 | tf_op jit(solution)/shard_map/all_gather | solution.py:145
  23.8 4.8 %collective-permute-start.2 = (bf16[512,128]{1,0:T(8,128)(2,1)S(1)}, bf16[512,128]{1,0:T(8,128)(2,1)S(1)}, u32[]{:S(2)}, u32[]{:S(2)}) collective-permute-start(bf16[512,128]{1,0:T(8,128)(2,1)S(1)} %get-tuple-element.555), channel_id=1, source_target_pairs={{4,0},{8,4},{12,8},{16,12},{20,16},{24,20},{28,24},{32,28},{36,32}... | collective-permute-start | bytes 393224 | tf_op jit(solution)/shard_map/ppermute | solution.py:14
  28.5 1.9 collective-permute-start.1
  30.5 1.9 collective-permute-start
  37.3 15.9 %while.83 = (s32[]{:T(128)}, f32[1024,128]{1,0:T(8,128)S(1)}, s32[2]{0:T(128)S(1)}, bf16[1024,128]{1,0:T(8,128)(2,1)S(1)}, s32[1024]{0:T(1024)S(1)}, /*index=5*/...) while((s32[]{:T(128)}, f32[1024,128]{1,0:T(8,128)S(1)}, ...), condition=%wide.region_11.12_spmd, body=%wide.region_8.11_spmd.sunk | while | flops 136905728 | bytes 1988110 | solution.py:88
  38.1 5.0 %while.86 = (s32[]{:T(128)}, f32[512,128]{1,0:T(8,128)S(1)}, s32[]{:T(128)}, s32[512]{0:T(512)S(1)}, s32[1024]{0:T(1024)S(1)}, /*index=5*/s32[]{:T(128)}, bf16[1...) while((s32[]{:T(128)}, f32[512,128]{1,0:T(8,128)S(1)}, ...), condition=%wide.region_10.10_spmd, body=%wide.region_9.9_spmd.sunk | while | flops 136905728 | bytes 935095 | solution.py:80
  40.1 1.8 convolution_add_fusion.7
  43.9 9.3 %while.86 = (s32[]{:T(128)}, f32[512,128]{1,0:T(8,128)S(1)}, s32[]{:T(128)}, s32[512]{0:T(512)S(1)}, s32[1024]{0:T(1024)S(1)}, /*index=5*/s32[]{:T(128)}, bf16[1...) while((s32[]{:T(128)}, f32[512,128]{1,0:T(8,128)S(1)}, ...), condition=%wide.region_10.10_spmd, body=%wide.region_9.9_spmd.sunk | while | flops 136905728 | bytes 935095 | solution.py:80
  45.8 1.8 convolution_add_fusion.7
  50.1 1.8 convolution_add_fusion.7
  53.2 3.8 collective-permute-start.3
  57.7 12.5 %all_gather.7 = bf16[512,512]{1,0:T(8,128)(2,1)S(1)} all-gather(bf16[512,128]{1,0:T(8,128)(2,1)S(1)} %copy-done.21), channel_id=1, replica_groups=mesh['dp'=64,'sub'=4] {'sub'}, dimensions={1}, use_global_device_ids=true | all-gather | bytes 655360 | tf_op jit(solution)/shard_map/all_gather | solution.py:146
  70.4 6.6 %psum.49 = f32[512]{0:T(512)S(1)} all-reduce(f32[512]{0:T(512)S(1)} %get-tuple-element.540), channel_id=1, replica_groups=mesh['dp'=64,'sub'=4] {'sub'}, use_global_device_ids=true, to_apply=%region_13.14 | all-reduce | flops 512 | bytes 4096 | tf_op jit(solution)/shard_map/psum | solution.py:201
  77.3 6.8 %psum.50 = f32[512]{0:T(512)S(1)} all-reduce(f32[512]{0:T(512)S(1)} %multiply_reduce_fusion.2), channel_id=1, replica_groups=mesh['dp'=64,'sub'=4] {'sub'}, use_global_device_ids=true, to_apply=%region_15.16 | all-reduce | flops 512 | bytes 4096 | tf_op jit(solution)/shard_map/psum | solution.py:203
  84.5 6.9 %all-reduce.1 = (f32[512]{0:T(512)S(1)}, f32[512]{0:T(512)S(1)}) all-reduce(f32[512]{0:T(512)S(1)} %get-tuple-element.453, f32[512]{0:T(512)S(1)} %get-tuple-element.452), channel_id=1, replica_groups=mesh['dp'=64,'sub'=4] {'sub'}, use_global_device_ids=true, to_apply=%region_20.21 | all-reduce | flops 1024 | bytes 8192 | tf_op jit(solution)/shard_map/psum | solution.py:218
  92.5 8.1 %collective-permute-start.4 = (bf16[512,128]{1,0:T(8,128)(2,1)S(1)}, bf16[512,128]{1,0:T(8,128)(2,1)S(1)}, u32[]{:S(2)}, u32[]{:S(2)}) collective-permute-start(bf16[512,128]{1,0:T(8,128)(2,1)S(1)} %get-tuple-element.551), channel_id=1, source_target_pairs={{4,0},{8,4},{12,8},{16,12},{20,16},{24,20},{28,24},{32,28},{36,32}... | collective-permute-start | bytes 393224 | tf_op jit(solution)/shard_map/ppermute | solution.py:14
  100.6 4.6 %collective-permute-done.4 = bf16[512,128]{1,0:T(8,128)(2,1)S(1)} collective-permute-done((bf16[512,128]{1,0:T(8,128)(2,1)S(1)}, bf16[512,128]{1,0:T(8,128)(2,1)S(1)}, u32[]{:S(2)}, u32[]{:S(2)}) %collective-permute-start.4) | collective-permute-done | bytes 131104 | tf_op jit(solution)/shard_map/ppermute | solution.py:14
  108.5 36.7 %while.85 = (s32[]{:T(128)}, f32[1024,128]{1,0:T(8,128)}, f32[1024,128]{1,0:T(8,128)}, f32[1024,128]{1,0:T(8,128)}, s32[2]{0:T(128)S(1)}, /*index=5*/bf16[1024,1...) while((s32[]{:T(128)}, f32[1024,128]{1,0:T(8,128)}, ...), condition=%wide.region_24.25_spmd, body=%wide.region_21.24_spmd.sunk | while | flops 342033408 | bytes 29520744 | solution.py:140
  110.1 10.7 %while.87 = (s32[]{:T(128)}, f32[512,128]{1,0:T(8,128)S(1)}, f32[1024,128]{1,0:T(8,128)}, f32[1024,128]{1,0:T(8,128)}, s32[]{:T(128)}, /*index=5*/s32[512]{0:T(5...) while((s32[]{:T(128)}, f32[512,128]{1,0:T(8,128)S(1)}, ...), condition=%wide.region_23.23_spmd, body=%wide.region_22.22_spmd.sunk | while | flops 342033408 | bytes 26108328 | solution.py:131
  123.4 20.8 %while.87 = (s32[]{:T(128)}, f32[512,128]{1,0:T(8,128)S(1)}, f32[1024,128]{1,0:T(8,128)}, f32[1024,128]{1,0:T(8,128)}, s32[]{:T(128)}, /*index=5*/s32[512]{0:T(5...) while((s32[]{:T(128)}, f32[512,128]{1,0:T(8,128)S(1)}, ...), condition=%wide.region_23.23_spmd, body=%wide.region_22.22_spmd.sunk | while | flops 342033408 | bytes 26108328 | solution.py:131
  146.5 2.1 collective-permute-start.7
  148.6 3.5 collective-permute-start.6
  152.1 1.9 collective-permute-start.5
  154.1 1.9 fusion.59
  156.0 2.3 collective-permute-done.5
  164.9 184.3 %all-reduce.7.cloned.1.call-done = (f32[512,512]{1,0:T(8,128)}, f32[128,512]{1,0:T(8,128)}) async-done(((f32[512,512]{1,0:T(8,128)}, f32[128,512]{1,0:T(8,128)}), (f32[512,512]{1,0:T(8,128)}, f32[128,512]{1,0:T(8,128)})) %all-reduce.7.cloned.1.call-update) | async-done | bytes 1310736 | tf_op jit(solution)/shard_map/psum | solution.py:254
  349.2 1.7 broadcast_multiply_fusion.1
  350.9 2.3 broadcast_multiply_fusion
  353.2 48.5 %all-reduce.5.cloned.1.call-done = f32[512,512]{1,0:T(8,128)} async-done(((f32[512,512]{1,0:T(8,128)}), f32[512,512]{1,0:T(8,128)}) %all-reduce.5.cloned.1.call-update) | async-done | bytes 1048592 | tf_op jit(solution)/shard_map/psum | solution.py:248
  401.7 1.7 fusion.54
  403.4 1.9 fusion.42
  405.3 25.9 %reduce-scatter.2.cloned.1.call-done = f32[512,128]{1,0:T(8,128)} async-done(((f32[512,512]{1,0:T(8,128)}), f32[512,128]{1,0:T(8,128)}) %reduce-scatter.2.cloned.1.call-update) | async-done | bytes 262160 | tf_op jit(solution)/shard_map/reduce_scatter | solution.py:207
  (211 shorter events, 53.3 us)
Async XLA Ops:
  7.2 15.0 %copy-start = (bf16[512,512]{1,0:T(8,128)(2,1)S(1)}, bf16[512,512]{1,0:T(8,128)(2,1)}, u32[]{:S(2)}) copy-start(bf16[512,512]{1,0:T(8,128)(2,1)} %param.15) | copy-start | bytes 1572868
  7.2 342.1 %all-reduce.7.cloned.1.call-start = ((), (), s32[]{:S(2)}) async-start(), calls=%async_computation.3 | async-start | bytes 2621440 | tf_op jit(solution)/shard_map/psum | solution.py:254
  23.8 12.7 %collective-permute-start.2 = (bf16[512,128]{1,0:T(8,128)(2,1)S(1)}, bf16[512,128]{1,0:T(8,128)(2,1)S(1)}, u32[]{:S(2)}, u32[]{:S(2)}) collective-permute-start(bf16[512,128]{1,0:T(8,128)(2,1)S(1)} %get-tuple-element.555), channel_id=1, source_target_pairs={{4,0},{8,4},{12,8},{16,12},{20,16},{24,20},{28,24},{32,28},{36,32}... | collective-permute-start | bytes 393224 | tf_op jit(solution)/shard_map/ppermute | solution.py:14
  28.5 8.7 %collective-permute-start.1 = (bf16[512,128]{1,0:T(8,128)(2,1)S(1)}, bf16[512,128]{1,0:T(8,128)(2,1)S(1)}, u32[]{:S(2)}, u32[]{:S(2)}) collective-permute-start(bf16[512,128]{1,0:T(8,128)(2,1)S(1)} %get-tuple-element.556), channel_id=1, source_target_pairs={{4,0},{8,4},{12,8},{16,12},{20,16},{24,20},{28,24},{32,28},{36,32}... | collective-permute-start | bytes 393224 | tf_op jit(solution)/shard_map/ppermute | solution.py:14
  30.5 6.8 %collective-permute-start = (bf16[512,128]{1,0:T(8,128)(2,1)S(1)}, bf16[512,128]{1,0:T(8,128)(2,1)S(1)}, u32[]{:S(2)}, u32[]{:S(2)}) collective-permute-start(bf16[512,128]{1,0:T(8,128)(2,1)S(1)} %get-tuple-element.557), channel_id=1, source_target_pairs={{4,0},{8,4},{12,8},{16,12},{20,16},{24,20},{28,24},{32,28},{36,32}... | collective-permute-start | bytes 393224 | tf_op jit(solution)/shard_map/ppermute | solution.py:14
  53.2 4.5 %copy-start.21 = (bf16[512,128]{1,0:T(8,128)(2,1)S(1)}, bf16[512,128]{1,0:T(8,128)(2,1)}, u32[]{:S(2)}) copy-start(bf16[512,128]{1,0:T(8,128)(2,1)} %param.17) | copy-start | bytes 393220
  53.2 16.9 %collective-permute-start.3 = (f32[512,128]{1,0:T(8,128)S(1)}, f32[512,128]{1,0:T(8,128)S(1)}, u32[]{:S(2)}, u32[]{:S(2)}) collective-permute-start(f32[512,128]{1,0:T(8,128)S(1)} %slice.39), channel_id=1, source_target_pairs={{0,4},{4,8},{8,12},{12,16},{16,20},{20,24},{24,28},{28,32},{32,36}... | collective-permute-start | bytes 786440 | tf_op jit(solution)/shard_map/ppermute | solution.py:14
  70.2 13.9 %copy-start.10 = (bf16[512,512]{1,0:T(8,128)(2,1)}, bf16[512,512]{1,0:T(8,128)(2,1)S(1)}, u32[]{:S(2)}) copy-start(bf16[512,512]{1,0:T(8,128)(2,1)S(1)} %all_gather.7) | copy-start | bytes 1572868
  77.0 7.1 %copy-start.19 = (bf16[128,512]{1,0:T(8,128)(2,1)S(1)}, bf16[128,512]{1,0:T(8,128)(2,1)}, u32[]{:S(2)}) copy-start(bf16[128,512]{1,0:T(8,128)(2,1)} %param.16) | copy-start | bytes 393220
  92.5 12.7 %collective-permute-start.4 = (bf16[512,128]{1,0:T(8,128)(2,1)S(1)}, bf16[512,128]{1,0:T(8,128)(2,1)S(1)}, u32[]{:S(2)}, u32[]{:S(2)}) collective-permute-start(bf16[512,128]{1,0:T(8,128)(2,1)S(1)} %get-tuple-element.551), channel_id=1, source_target_pairs={{4,0},{8,4},{12,8},{16,12},{20,16},{24,20},{28,24},{32,28},{36,32}... | collective-permute-start | bytes 393224 | tf_op jit(solution)/shard_map/ppermute | solution.py:14
  108.5 1.6 copy-start.6
  110.7 1.8 copy-start.4
  114.4 2.7 copy-start.29
  118.1 1.6 copy-start.5
  121.8 1.6 copy-start.6
  124.0 1.8 copy-start.4
  127.7 2.7 copy-start.29
  131.4 1.6 copy-start.5
  134.1 1.8 copy-start.4
  137.8 2.7 copy-start.29
  141.6 1.6 copy-start.5
  146.3 7.7 %copy-start.11 = (bf16[512,512]{1,0:T(8,128)(2,1)S(1)}, bf16[512,512]{1,0:T(8,128)(2,1)}, u32[]{:S(2)}) copy-start(bf16[512,512]{1,0:T(8,128)(2,1)} %copy-done.10) | copy-start | bytes 1572868
  146.5 11.7 %copy-start.14 = (f32[1024,128]{1,0:T(8,128)S(1)}, f32[1024,128]{1,0:T(8,128)}, u32[]{:S(2)}) copy-start(f32[1024,128]{1,0:T(8,128)} %get-tuple-element.447) | copy-start | bytes 1572868
  146.5 9.4 %collective-permute-start.7 = (f32[512,128]{1,0:T(8,128)S(1)}, f32[512,128]{1,0:T(8,128)S(1)}, u32[]{:S(2)}, u32[]{:S(2)}) collective-permute-start(f32[512,128]{1,0:T(8,128)S(1)} %slice.46), channel_id=1, source_target_pairs={{0,4},{4,8},{8,12},{12,16},{16,20},{20,24},{24,28},{28,32},{32,36}... | collective-permute-start | bytes 786440 | tf_op jit(solution)/shard_map/ppermute | solution.py:14
  148.6 7.4 %collective-permute-start.6 = (f32[512,128]{1,0:T(8,128)S(1)}, f32[512,128]{1,0:T(8,128)S(1)}, u32[]{:S(2)}, u32[]{:S(2)}) collective-permute-start(f32[512,128]{1,0:T(8,128)S(1)} %slice.44), channel_id=1, source_target_pairs={{0,4},{4,8},{8,12},{12,16},{16,20},{20,24},{24,28},{28,32},{32,36}... | collective-permute-start | bytes 786440 | tf_op jit(solution)/shard_map/ppermute | solution.py:14
  152.1 6.1 %collective-permute-start.5 = (f32[512,128]{1,0:T(8,128)S(1)}, f32[512,128]{1,0:T(8,128)S(1)}, u32[]{:S(2)}, u32[]{:S(2)}) collective-permute-start(f32[512,128]{1,0:T(8,128)S(1)} %slice.42), channel_id=1, source_target_pairs={{0,4},{4,8},{8,12},{12,16},{16,20},{20,24},{24,28},{28,32},{32,36}... | collective-permute-start | bytes 786440 | tf_op jit(solution)/shard_map/ppermute | solution.py:14
  156.0 2.4 copy-start.17
  156.0 2.5 copy-start.18
  161.1 240.6 %all-reduce.5.cloned.1.call-start = ((), (), s32[]{:S(2)}) async-start(), calls=%async_computation.2 | async-start | bytes 2097152 | tf_op jit(solution)/shard_map/psum | solution.py:248
  162.7 268.6 %reduce-scatter.2.cloned.1.call-start = ((), (), s32[]{:S(2)}) async-start(), calls=%async_computation.1 | async-start | bytes 1310720 | tf_op jit(solution)/shard_map/reduce_scatter | solution.py:207
  353.2 50.2 %copy-start.22 = (bf16[512,128]{1,0:T(8,128)(2,1)S(1)}, bf16[512,128]{1,0:T(8,128)(2,1)}, u32[]{:S(2)}) copy-start(bf16[512,128]{1,0:T(8,128)(2,1)} %param.17) | copy-start | bytes 393220
  403.4 27.8 %copy-start.23 = (bf16[512,128]{1,0:T(8,128)(2,1)S(1)}, bf16[512,128]{1,0:T(8,128)(2,1)}, u32[]{:S(2)}) copy-start(bf16[512,128]{1,0:T(8,128)(2,1)} %param.13) | copy-start | bytes 393220
  (25 other events, 25.0 us)
Sparse Core Ops, SparseCore 0:
  161.2 187.9 all-reduce.6
  351.7 49.9 all-reduce.4
  404.2 26.9 reduce-scatter.1
where the time goes:
time: 441 us; the launch traced here: 439 us
  waiting for transfers between devices  266 us (60%)
  blocking collectives  47 us (11%)
  matrix products  28.9 us (7%)
  starting transfers between devices  28.1 us (6%)
  local copies, waits for them, and re-layouts  21 us (5%)
  other arithmetic  18 us (4%)
  loops' own time  16.7 us (4%)
  between operations  14.1 us (3%)
    psum x1, waiting for transfers between devices, shards(): total_win, total_wout = lax.psum((grad_win, grad_wout), 'dp')  184 us
    psum x1, waiting for transfers between devices, shards(): summed_input = lax.psum(d_input, 'sub')  48.5 us
    ppermute x8, starting transfers between devices, shifted(): return lax.ppermute(value, axis, pairs)  28 us
    reduce_scatter x1, waiting for transfers between devices, shards(): lax.psum_scatter(jnp.dot(gated_rows, weight_out, preferred_element_type=j...  25.9 us
    all_gather x1, blocking collectives, shards(): lax.all_gather(tokens, 'sub', axis=1, tiled=True)  14.1 us
    all_gather x1, blocking collectives, shards(): lax.all_gather(grad_out, 'sub', axis=1, tiled=True)  12.5 us
    dot_general x8, matrix products, contract_cols(): lax.dot_general(left_op, right_op, (((1,), (1,)), ((), ())), preferred_el...  10.5 us
  transfers between devices with their start and end apart: 11, of which 5 were waited for; matrix products, arithmetic and copies ran while one was open for 4% of the time, Pallas kernels for 0%

commit v1 on v0

v1 whole, which is shorter than its diff:
```python
import functools
import math

import jax
import jax.numpy as jnp
from jax import lax
from jax.experimental import pallas as pl
from jax.experimental.pallas import tpu as pltpu
from jax.sharding import PartitionSpec as P

EPSILON = 1e-05
NX, NZ, NC, NY = 4, 8, 2, 4
ROWS, HEAD, WIDTH = 512, 128, 512
TILE = 128
MESH = pl.DeviceIdType.MESH
BF, F32 = jnp.bfloat16, jnp.float32

NN = (((1,), (0,)), ((), ()))
NT = (((1,), (1,)), ((), ()))
TN = (((0,), (0,)), ((), ()))


def mm(left, right, dims=NN):
    return lax.dot_general(left, right, dims, preferred_element_type=F32)


class Sender:
    def __init__(self, send_sem, recv_sem):
        self.send_sem, self.recv_sem, self.copies = send_sem, recv_sem, []

    def __call__(self, src, dst, device):
        i = len(self.copies)
        copy = pltpu.make_async_remote_copy(
            src_ref=src,
            dst_ref=dst,
            send_sem=self.send_sem.at[i],
            recv_sem=self.recv_sem.at[i],
            device_id=device,
            device_id_type=MESH,
        )
        copy.start()
        self.copies.append(copy)
        return copy


class Reduce:
    def __init__(self, send, place, refs, scale):
        self.send, self.scale = send, scale
        self.x, self.z, self.c, self.at = place
        self.part, self.sb, self.rc, self.sx, self.rx, self.sz, self.rz, self.full = refs
        self.dt = self.full.dtype

    def s1(self):
        c = self.c
        self.sb[...] = self.part[1 - c].astype(self.dt)
        self.w1 = self.send(self.sb, self.rc, self.at(self.x, self.z, 1 - c))

    def s2(self):
        self.w1.wait_recv()
        total = self.part[self.c] + self.rc[...].astype(F32)
        self.part[self.c] = total
        self.sx[...] = total.astype(self.dt)
        self.w2 = []
        for r in (1, 3, 2):
            to = lax.rem(self.x + r, NX)
            self.w2.append(
                self.send(self.sx.at[to], self.rx.at[r - 1], self.at(to, self.z, self.c))
            )

    def s3(self):
        for w in self.w2:
            w.wait_recv()
        total = self.part[self.c, self.x]
        for r in range(NX - 1):
            total = total + self.rx[r].astype(F32)
        self.part[self.c, self.x] = total
        self.sz[...] = total.astype(self.dt)
        self.w3 = []
        for r in (1, 7, 2, 6, 3, 5, 4):
            to = lax.rem(self.z + r, NZ)
            self.w3.append(
                self.send(self.sz.at[to], self.rz.at[r - 1], self.at(self.x, to, self.c))
            )

    def s4(self):
        for w in self.w3:
            w.wait_recv()
        total = self.part[self.c, self.x, self.z]
        for r in range(NZ - 1):
            total = total + self.rz[r].astype(F32)
        mine = (self.c, self.x, self.z)
        self.full[mine] = (total * self.scale).astype(self.dt)
        self.w4 = []
        for r in (1, 7, 2, 6, 3, 5, 4):
            to = lax.rem(self.z + r, NZ)
            self.w4.append(
                self.send(self.full.at[mine], self.full.at[mine], self.at(self.x, to, self.c))
            )

    def s5(self):
        for w in self.w4:
            w.wait_recv()
        mine = (self.c, self.x)
        self.w5 = []
        for r in (1, 3, 2):
            to = lax.rem(self.x + r, NX)
            self.w5.append(
                self.send(self.full.at[mine], self.full.at[mine], self.at(to, self.z, self.c))
            )

    def s6(self):
        for w in self.w5:
            w.wait_recv()
        self.w6 = self.send(
            self.full.at[self.c], self.full.at[self.c], self.at(self.x, self.z, 1 - self.c)
        )

    def s7(self):
        self.w6.wait_recv()


def column(value):
    return jnp.sum(value, axis=1, keepdims=True)


def start_rows(lens_ref, first_row):
    lens = jnp.broadcast_to(lens_ref[...].astype(F32), (128, 128))
    down = lax.broadcasted_iota(jnp.int32, (128, 128), 0)
    across = lax.broadcasted_iota(jnp.int32, (128, 128), 1)
    as_column = column(jnp.where(down == across, lens, 0.0))
    starts = jnp.sum(jnp.where(down < across, as_column, 0.0), axis=0, keepdims=True)
    rows = (first_row + lax.broadcasted_iota(jnp.int32, (ROWS, 128), 0)).astype(F32)
    own = jnp.max(jnp.where(starts <= rows, starts, 0.0), axis=1, keepdims=True)
    return own - first_row.astype(F32)


def kernel(
    tok, lens, win, wout, gout,
    lo, gt, gwin, gwout,
    xg, gg, wc, xh, xo, xn, xnt, xr, proj, slope, kv, srow,
    w_own, w_prev, sl_own, sl_prev, ds_own, ds_prev,
    stat, gat, datt, dgate, dq, dk, dv, dkv_s, dkv_r,
    din, din_s, din_r, stat2, dhid,
    *rest,
):
    reduce_refs, (send_sem, recv_sem) = rest[:-2], rest[-2:]
    d, y = lax.axis_index("dp"), lax.axis_index("sub")
    c = lax.rem(d, NC)
    z = lax.rem(d // NC, NZ)
    x = d // (NC * NZ)
    ndp = NX * NZ * NC

    def at(ax, az, ac):
        return ((ax * NZ + az) * NC + ac, y)

    above = (lax.rem(d + 1, ndp), y)
    below = (lax.rem(d + ndp - 1, ndp), y)
    y_peers = [(r, lax.rem(y + r, NY)) for r in (1, 3, 2)]

    barrier = pltpu.get_barrier_semaphore()
    greet = [(d, peer) for _, peer in y_peers]
    greet += [at(lax.rem(x + r, NX), z, c) for r in range(1, NX)]
    greet += [at(x, lax.rem(z + r, NZ), c) for r in range(1, NZ)]
    greet += [at(x, z, 1 - c)]
    greet += [(lax.rem(d + ndp + 2 * c - 1, ndp), y)]
    for device in greet:
        pl.semaphore_signal(barrier, inc=1, device_id=device, device_id_type=MESH)
    pl.semaphore_wait(barrier, len(greet))

    send = Sender(send_sem, recv_sem)
    place = (x, z, c, at)
    scaling = 1.0 / math.sqrt(ROWS * ndp)
    sums = [Reduce(send, place, reduce_refs[8 * i : 8 * i + 8], scaling) for i in range(3)]
    r_out, r_uq, r_vk = sums

    got_x = [send(tok, xg.at[y], (d, peer)) for _, peer in y_peers]
    got_g = [send(gout, gg.at[y], (d, peer)) for _, peer in y_peers]
    got_w = [
        send(
            wout.at[:, pl.ds(pl.multiple_of(peer * HEAD, HEAD), HEAD)],
            wc.at[y],
            (d, peer),
        )
        for _, peer in y_peers
    ]
    xg[y] = tok[...]
    gg[y] = gout[...]
    wc[y] = wout[:, pl.ds(pl.multiple_of(y * HEAD, HEAD), HEAD)]
    srow[...] = jnp.broadcast_to(start_rows(lens, d * ROWS), (ROWS, 128))
    for w in got_x:
        w.wait_recv()

    @pl.loop(0, ROWS // TILE)
    def _(t):
        rows = pl.ds(pl.multiple_of(t * TILE, TILE), TILE)
        parts = [xg[b, rows, :].astype(F32) for b in range(NY)]
        mean = column(parts[0] + parts[1] + parts[2] + parts[3]) * (1.0 / WIDTH)
        parts = [part - mean for part in parts]
        var = column(sum(part * part for part in parts)) * (1.0 / WIDTH)
        inv = lax.rsqrt(var + EPSILON)
        xr[rows, :] = jnp.broadcast_to(inv, (TILE, 128))
        for b in range(NY):
            hat = parts[b] * inv
            xh[b, rows, :] = hat
            xn[rows, b * HEAD : (b + 1) * HEAD] = hat.astype(BF)

    def project(g):
        hidden = mm(xn[...], win[:, g * HEAD : (g + 1) * HEAD])
        sig = 0.5 * jnp.tanh(0.5 * hidden) + 0.5
        proj[g] = (hidden * sig).astype(BF)
        slope[g] = sig * (1.0 + hidden * (1.0 - sig))

    project(3)
    got_k = send(proj.at[3], kv.at[1], above)
    project(1)
    got_v = send(proj.at[1], kv.at[0], above)
    project(2)

    root = 1.0 / math.sqrt(HEAD)

    def attend(q_rows, k_rows, t, width, shift, causal):
        scores = mm(q_rows, k_rows, NT) * root
        col = lax.broadcasted_iota(jnp.int32, (TILE, width), 1)
        begin = srow[t * TILE : (t + 1) * TILE, 0:1].astype(jnp.int32) + shift
        allowed = col >= begin
        if causal:
            row = lax.broadcasted_iota(jnp.int32, (TILE, width), 0) + t * TILE
            allowed = allowed & (col <= row)
        sig = 0.5 * jnp.tanh(0.5 * scores) + 0.5
        weight = jnp.where(allowed, scores * sig, 0.0).astype(BF)
        tangent = jnp.where(allowed, sig * (1.0 + scores * (1.0 - sig)) * root, 0.0)
        return weight, tangent

    for t in range(ROWS // TILE):
        rows, n = slice(t * TILE, (t + 1) * TILE), (t + 1) * TILE
        weight, tangent = attend(proj[2, rows], proj[3, :n], t, n, 0, True)
        w_own[rows, :n] = weight
        sl_own[rows, :n] = tangent
        din[0, rows] = mm(weight, proj[1, :n])

    project(0)
    for w in got_g:
        w.wait_recv()
    gate = proj[0].astype(F32)
    d_gated = sum(
        mm(gg[b], wout[:, b * HEAD : (b + 1) * HEAD], NT) for b in range(NY)
    )
    dgate[...] = d_gated
    e = d_gated * gate
    din[1] = e

    got_k.wait_recv()
    got_v.wait_recv()
    for t in range(ROWS // TILE):
        rows = slice(t * TILE, (t + 1) * TILE)
        weight, tangent = attend(proj[2, rows], kv[1], t, ROWS, ROWS, False)
        w_prev[rows, :] = weight
        sl_prev[rows, :] = tangent
        din[0, rows] = din[0, rows] + mm(weight, kv[0])

    a = din[0]
    e = din[1]
    sum_a = column(a)
    ca = a - sum_a * (1.0 / HEAD)
    lane = lax.broadcasted_iota(jnp.int32, (ROWS, 128), 1)
    packed = jnp.where(
        lane == 0, sum_a,
        jnp.where(lane == 1, column(ca * ca),
                  jnp.where(lane == 2, column(e), jnp.where(lane == 3, column(e * ca), 0.0))),
    )
    stat[y] = packed.T[:8]
    got_s = [send(stat.at[y], stat.at[y], (d, peer)) for _, peer in y_peers]
    xnt[...] = xn[...].T
    for w in got_s:
        w.wait_recv()
    heads = [stat[h] for h in range(NY)]
    mean = sum(h[0:1] for h in heads) * (1.0 / WIDTH)
    var, s_e, s_en = 0.0, 0.0, 0.0
    for h in heads:
        off = h[0:1] * (1.0 / HEAD) - mean
        var = var + h[1:2] + HEAD * off * off
        s_e = s_e + h[2:3]
        s_en = s_en + h[3:4] + off * h[2:3]
    inv = lax.rsqrt(var * (1.0 / WIDTH) + EPSILON)
    line = lax.broadcasted_iota(jnp.int32, (128, ROWS), 0)
    back = jnp.where(
        line == 0, mean,
        jnp.where(line == 1, inv,
                  jnp.where(line == 2, s_e * (1.0 / WIDTH),
                            jnp.where(line == 3, s_en * inv * (1.0 / WIDTH), 0.0))),
    ).T
    mean, inv, s_e, s_en = [back[:, i : i + 1] for i in range(4)]
    normed = (din[0] - mean) * inv
    datt[...] = (inv * (din[1] - s_e - normed * s_en)).astype(BF)
    gat[y] = (normed * proj[0].astype(F32)).astype(BF)
    got_a = [send(gat.at[y], gat.at[y], (d, peer)) for _, peer in y_peers]
    dhid[:, 0:HEAD] = (dgate[...] * normed * slope[0]).astype(BF)

    for t in range(ROWS // TILE):
        rows = slice(t * TILE, (t + 1) * TILE)
        ds = (mm(datt[rows], kv[0], NT) * sl_prev[rows, :]).astype(BF)
        ds_prev[rows, :] = ds
        dq[rows, :] = mm(ds, kv[1])
    dkv_s[0] = mm(w_prev[...], datt[...], TN).astype(BF)
    got_dv = send(dkv_s.at[0], dkv_r.at[0], below)
    dkv_s[1] = mm(ds_prev[...], proj[2], TN).astype(BF)
    got_dk = send(dkv_s.at[1], dkv_r.at[1], below)

    gated = gat[y]
    gated_t = gated.T
    for b in range(NY):
        r_out.part[b // 2, (b % 2) * 2 : (b % 2) * 2 + 2] = mm(gated_t, gg[b]).reshape(2, NZ, 8, HEAD)
    r_out.s1()

    for t in range(ROWS // TILE):
        rows, n = slice(t * TILE, (t + 1) * TILE), (t + 1) * TILE
        ds = (mm(datt[rows], proj[1, :n], NT) * sl_own[rows, :n]).astype(BF)
        ds_own[rows, :n] = ds
        dq[rows, :] = dq[rows, :] + mm(ds, proj[3, :n])
    dhid[:, 2 * HEAD : 3 * HEAD] = (dq[...] * slope[2]).astype(BF)
    for i, g in enumerate((0, 2)):
        r_uq.part[i] = mm(xnt[...], dhid[:, g * HEAD : (g + 1) * HEAD]).reshape(NX, NZ, 16, HEAD)
    r_uq.s1()
    r_out.s2()
    for t in range(ROWS // TILE):
        cols = slice(t * TILE, (t + 1) * TILE)
        dk[cols, :] = mm(ds_own[t * TILE :, cols], proj[2, t * TILE :], TN)
        dv[cols, :] = mm(w_own[t * TILE :, cols], datt[t * TILE :], TN)
    r_uq.s2()
    got_dv.wait_recv()
    dhid[:, HEAD : 2 * HEAD] = ((dv[...] + dkv_r[0].astype(F32)) * slope[1]).astype(BF)
    got_dk.wait_recv()
    dhid[:, 3 * HEAD :] = ((dk[...] + dkv_r[1].astype(F32)) * slope[3]).astype(BF)
    for i, g in enumerate((1, 3)):
        r_vk.part[i] = mm(xnt[...], dhid[:, g * HEAD : (g + 1) * HEAD]).reshape(NX, NZ, 16, HEAD)
    r_vk.s1()

    one, two = 0.0, 0.0
    for b in range(NY):
        part = mm(dhid[...], win[b * HEAD : (b + 1) * HEAD, :], NT)
        one = one + part
        two = two + part * xh[b]
        din[b] = part
        din_s[b] = part.astype(BF)
    packed = jnp.where(lane == 0, column(one), jnp.where(lane == 1, column(two), 0.0))
    stat2[y] = packed.T[:8]
    got_i = [send(din_s.at[peer], din_r.at[r - 1], (d, peer)) for r, peer in y_peers]
    got_t = [send(stat2.at[y], stat2.at[y], (d, peer)) for _, peer in y_peers]
    r_uq.s3()
    r_vk.s2()
    r_out.s3()

    for w in got_a + got_w:
        w.wait_recv()
    lo[...] = (
        tok[...].astype(F32) + sum(mm(gat[h], wc[h]) for h in range(NY))
    ).astype(BF)

    r_uq.s4()
    r_vk.s3()
    r_out.s4()
    r_uq.s5()
    r_vk.s4()
    r_out.s5()

    for w in got_i + got_t:
        w.wait_recv()
    total = din[y]
    for r in range(NY - 1):
        total = total + din_r[r].astype(F32)
    both = (stat2[0] + stat2[1] + stat2[2] + stat2[3]) * (1.0 / WIDTH)
    back = jnp.where(line == 0, both[0:1], jnp.where(line == 1, both[1:2], 0.0)).T
    piece = xr[:, 0:1] * (total - back[:, 0:1] - xh[y] * back[:, 1:2])
    gt[...] = (gout[...].astype(F32) + piece).astype(BF)

    r_uq.s6()
    r_vk.s5()
    r_out.s6()
    r_uq.s7()
    r_vk.s6()
    for i, g in enumerate((0, 2)):
        gwin[:, g * HEAD : (g + 1) * HEAD] = r_uq.full[i].reshape(ROWS, HEAD).astype(F32)
    r_out.s7()
    for b in range(NY):
        block = r_out.full[b // 2, (b % 2) * 2 : (b % 2) * 2 + 2]
        gwout[:, b * HEAD : (b + 1) * HEAD] = block.reshape(HEAD, HEAD)
    r_vk.s7()
    for i, g in enumerate((1, 3)):
        gwin[:, g * HEAD : (g + 1) * HEAD] = r_vk.full[i].reshape(ROWS, HEAD).astype(F32)
    for w in send.copies:
        w.wait_send()


def reduce_scratch(rows, dt):
    return [
        pltpu.VMEM((NC, NX, NZ, rows, HEAD), F32),
        pltpu.VMEM((NX, NZ, rows, HEAD), dt),
        pltpu.VMEM((NX, NZ, rows, HEAD), dt),
        pltpu.VMEM((NX, NZ, rows, HEAD), dt),
        pltpu.VMEM((NX - 1, NZ, rows, HEAD), dt),
        pltpu.VMEM((NZ, rows, HEAD), dt),
        pltpu.VMEM((NZ - 1, rows, HEAD), dt),
        pltpu.VMEM((NC, NX, NZ, rows, HEAD), dt),
    ]


def shards(tokens, lengths, weight_in, weight_out, grad_out):
    lengths = lengths.reshape(1, -1)
    vm = pl.BlockSpec(memory_space=pltpu.VMEM)
    blocks = lambda n, dt: pltpu.VMEM((n, ROWS, HEAD), dt)
    full = lambda dt: pltpu.VMEM((ROWS, WIDTH), dt)
    one = lambda dt: pltpu.VMEM((ROWS, HEAD), dt)
    scratch = [
        blocks(NY, BF), blocks(NY, BF), pltpu.VMEM((NY, HEAD, HEAD), BF),
        blocks(NY, F32), one(F32), full(BF), full(BF), one(F32),
        blocks(4, BF), blocks(4, F32), blocks(2, BF), one(F32),
        full(BF), full(BF), full(F32), full(F32), full(BF), full(BF),
        pltpu.VMEM((NY, 8, ROWS), F32), blocks(NY, BF), one(BF), one(F32),
        one(F32), one(F32), one(F32), blocks(2, BF), blocks(2, BF),
        blocks(NY, F32), blocks(NY, BF), blocks(NY - 1, BF),
        pltpu.VMEM((NY, 8, ROWS), F32), full(BF),
        *reduce_scratch(8, F32), *reduce_scratch(16, BF), *reduce_scratch(16, BF),
        pltpu.SemaphoreType.DMA((100,)), pltpu.SemaphoreType.DMA((100,)),
    ]
    return pl.pallas_call(
        kernel,
        out_shape=(
            jax.ShapeDtypeStruct((ROWS, HEAD), BF),
            jax.ShapeDtypeStruct((ROWS, HEAD), BF),
            jax.ShapeDtypeStruct((WIDTH, 4 * HEAD), F32),
            jax.ShapeDtypeStruct((HEAD, WIDTH), F32),
        ),
        in_specs=[vm] * 5,
        out_specs=(vm,) * 4,
        scratch_shapes=scratch,
        compiler_params=pltpu.CompilerParams(
            collective_id=0, has_side_effects=True, vmem_limit_bytes=48 * 1024 * 1024
        ),
        name="layer",
    )(tokens, lengths, weight_in, weight_out, grad_out)


def solution(mesh):
    placed = (P("dp", "sub"), P(), P(None, "sub"), P("sub", None), P("dp", "sub"))
    return jax.shard_map(
        shards,
        mesh=mesh,
        in_specs=placed,
        out_specs=(P("dp", "sub"), P("dp", "sub"), P(None, "sub"), P("sub", None)),
        check_vma=False,
    )
```

time: 441 us -> 69.6 us (0.16)
  waiting for transfers between devices: 266 us -> 0 us
  Pallas kernels: 0 us -> 61.3 us
  blocking collectives: 47 us -> 0 us
  matrix products: 28.9 us -> 0 us
  starting transfers between devices: 28.1 us -> 0 us
  other arithmetic: 18 us -> 0 us
  loops' own time: 16.7 us -> 0 us
  local copies, waits for them, and re-layouts: 21 us -> 7.38 us
  between operations: 14.1 us -> 0.65 us
    psum x2 -> x0, waiting for transfers between devices: 233 us -> none  [the longest x1 184 us: shards(): total_win, total_wout = lax.psum((grad_win, grad_wout), 'dp')]
    pallas_call x0 -> x1, Pallas kernels: none -> 61.3 us  [shards(): pl.pallas_call(kernel, out_shape=(jax.ShapeDtypeStruct((ROWS, HEAD), BF),...]
    dot_general x24 -> x0, matrix products: 28.9 us -> none  [the longest x8 10.5 us: contract_cols(): lax.dot_general(left_op, right_op, (((1,), (1,)), ((), ())), preferred_el...]
    ppermute x8 -> x0, starting transfers between devices: 28 us -> none  [shifted(): return lax.ppermute(value, axis, pairs)]
    all_gather x2 -> x0, blocking collectives: 26.6 us -> none  [the longest x1 14.1 us: shards(): lax.all_gather(tokens, 'sub', axis=1, tiled=True)]
    reduce_scatter x1 -> x0, waiting for transfers between devices: 25.9 us -> none  [shards(): lax.psum_scatter(jnp.dot(gated_rows, weight_out, preferred_element_type=j...]
    psum x3 -> x0, blocking collectives: 20.4 us -> none  [the longest x1 6.93 us: shards(): lax.psum((jnp.sum(d_normed, 1), jnp.sum(d_normed * normed, 1)), 'sub')]
    another operation x6 -> x0, loops' own time: 16.7 us -> none  [the longest x2 8.64 us: per_query(): lax.fori_loop(first_block[query_block], query_block + 1, per_key, jnp.zer...]
  transfers between devices with their start and end apart: 11 -> 0, of which waited for: 5 -> 0; matrix products, arithmetic and copies ran while one was open for 4% -> 0% of each run, Pallas kernels for 0% -> 0%
where the time goes in v1:
time: 69.6 us; the launch traced here: 69.4 us
  Pallas kernels  61.3 us (88%)
  local copies, waits for them, and re-layouts  7.38 us (11%)
    pallas_call x1, Pallas kernels, shards(): pl.pallas_call(kernel, out_shape=(jax.ShapeDtypeStruct((ROWS, HEAD), BF),...  61.3 us
    unnamed x14, local copies, waits for them, and re-layouts  7.38 us

profile of v1, /device:TPU:1, one launch (start us, length us, event | category | flops | bytes accessed | tf_op | source)
XLA Modules:
  0.0 69.4 jit_solution(17825600237239461909)
XLA Ops:
  0.6 0.0 copy-start.4
  0.6 0.6 copy-done.4
  1.3 0.0 copy-start
  1.3 1.0 %copy-done = bf16[512,512]{1,0:T(8,128)(2,1)S(1)} copy-done((bf16[512,512]{1,0:T(8,128)(2,1)S(1)}, bf16[512,512]{1,0:T(8,128)(2,1)}, u32[]{:S(2)}) %copy-start) | copy-done | bytes 524312
  2.3 0.0 copy-start.1
  2.3 0.9 %copy-done.1 = bf16[512,128]{1,0:T(8,128)(2,1)S(1)} copy-done((bf16[512,128]{1,0:T(8,128)(2,1)S(1)}, bf16[512,128]{1,0:T(8,128)(2,1)}, u32[]{:S(2)}) %copy-start.1) | copy-done | bytes 131096
  3.2 0.0 copy-start.2
  3.2 0.9 %copy-done.2 = bf16[128,512]{1,0:T(8,128)(2,1)S(1)} copy-done((bf16[128,512]{1,0:T(8,128)(2,1)S(1)}, bf16[128,512]{1,0:T(8,128)(2,1)}, u32[]{:S(2)}) %copy-start.2) | copy-done | bytes 131096
  4.1 0.0 copy-start.3
  4.1 0.9 %copy-done.3 = bf16[512,128]{1,0:T(8,128)(2,1)S(1)} copy-done((bf16[512,128]{1,0:T(8,128)(2,1)S(1)}, bf16[512,128]{1,0:T(8,128)(2,1)}, u32[]{:S(2)}) %copy-start.3) | copy-done | bytes 131096
  5.0 61.3 %layer.1 = (bf16[512,128]{1,0:T(8,128)(2,1)S(1)}, bf16[512,128]{1,0:T(8,128)(2,1)S(1)}, f32[512,512]{1,0:T(8,128)S(1)}, f32[128,512]{1,0:T(8,128)S(1)}) custom-call(bf16[512,128]{1,0:T(8,128)(2,1)S(1)} %copy-done.1, s32[1,128]{1,0:T(1,128)S(1)} %bitcast.1, bf16[512,512]{1,0:T(8,128)(2,1)S(1)} %copy-done, bf16[128,512]{1,0:T(8,128)(2,1)S(1)} %copy-done.2, ...), custom_call_target="tpu_custom_call" | custom-call | tf_op jit(solution)/shard_map/layer/pallas_call | solution.py:425
  66.4 0.7 copy.13
  67.0 0.7 copy.14
  67.7 1.0 %copy.15 = f32[512,512]{1,0:T(8,128)} copy(f32[512,512]{1,0:T(8,128)S(1)} %get-tuple-element.10) | data formatting | bytes 2097152
  68.7 0.7 %copy.16 = f32[128,512]{1,0:T(8,128)} copy(f32[128,512]{1,0:T(8,128)S(1)} %get-tuple-element.11) | data formatting | bytes 524288
Async XLA Ops:
  0.6 0.7 copy-start.4
  1.3 1.0 %copy-start = (bf16[512,512]{1,0:T(8,128)(2,1)S(1)}, bf16[512,512]{1,0:T(8,128)(2,1)}, u32[]{:S(2)}) copy-start(bf16[512,512]{1,0:T(8,128)(2,1)} %win.1) | copy-start | bytes 1572868
  2.3 0.9 %copy-start.1 = (bf16[512,128]{1,0:T(8,128)(2,1)S(1)}, bf16[512,128]{1,0:T(8,128)(2,1)}, u32[]{:S(2)}) copy-start(bf16[512,128]{1,0:T(8,128)(2,1)} %tok.1) | copy-start | bytes 393220
  3.2 0.9 %copy-start.2 = (bf16[128,512]{1,0:T(8,128)(2,1)S(1)}, bf16[128,512]{1,0:T(8,128)(2,1)}, u32[]{:S(2)}) copy-start(bf16[128,512]{1,0:T(8,128)(2,1)} %wout.1) | copy-start | bytes 393220
  4.1 0.9 %copy-start.3 = (bf16[512,128]{1,0:T(8,128)(2,1)S(1)}, bf16[512,128]{1,0:T(8,128)(2,1)}, u32[]{:S(2)}) copy-start(bf16[512,128]{1,0:T(8,128)(2,1)} %gout.1) | copy-start | bytes 393220

commit v2 on v1

v2 whole, which is shorter than its diff:
```python
import functools
import math

import jax
import jax.numpy as jnp
from jax import lax
from jax.experimental import pallas as pl
from jax.experimental.pallas import tpu as pltpu
from jax.sharding import PartitionSpec as P

EPSILON = 1e-05
NX, NZ, NC, NY = 4, 8, 2, 4
ROWS, HEAD, WIDTH = 512, 128, 512
TILE = 128
MESH = pl.DeviceIdType.MESH
BF, F32 = jnp.bfloat16, jnp.float32

NN = (((1,), (0,)), ((), ()))
NT = (((1,), (1,)), ((), ()))
TN = (((0,), (0,)), ((), ()))


def mm(left, right, dims=NN):
    return lax.dot_general(left, right, dims, preferred_element_type=F32)


class Sender:
    def __init__(self, send_sem, recv_sem):
        self.send_sem, self.recv_sem, self.copies = send_sem, recv_sem, []

    def __call__(self, src, dst, device):
        i = len(self.copies)
        copy = pltpu.make_async_remote_copy(
            src_ref=src,
            dst_ref=dst,
            send_sem=self.send_sem.at[i],
            recv_sem=self.recv_sem.at[i],
            device_id=device,
            device_id_type=MESH,
        )
        copy.start()
        self.copies.append(copy)
        return copy


class Reduce:
    def __init__(self, send, core, first, second, refs, scale):
        self.send, self.scale = send, scale
        self.c, self.core = core
        self.n1, self.i1, self.at1 = first
        self.n2, self.i2, self.at2 = second
        self.part, self.sb, self.rc, self.s_1, self.r_1, self.s_2, self.r_2, self.full = refs
        self.dt = self.full.dtype

    @staticmethod
    def far_first(n):
        return sorted(range(1, n), key=lambda r: (-min(r, n - r), r))

    def to1(self, r):
        return lax.rem(self.i1 + r, self.n1)

    def to2(self, r):
        return lax.rem(self.i2 + r, self.n2)

    def s1(self, other):
        self.sb[...] = other.astype(self.dt).reshape(self.sb.shape)
        self.w1 = self.send(self.sb, self.rc, self.core)

    def keep(self, own):
        self.part[...] = own.reshape(self.part.shape)

    def s2(self):
        self.w1.wait_recv()
        total = self.part[...] + self.rc[...].astype(F32)
        self.part[...] = total
        self.s_1[...] = total.astype(self.dt)
        self.w2 = []
        for r in self.far_first(self.n1):
            to = self.to1(r)
            self.w2.append(self.send(self.s_1.at[to], self.r_1.at[r - 1], self.at1(to)))

    def s3(self):
        for w in self.w2:
            w.wait_recv()
        total = self.part[self.i1]
        for r in range(self.n1 - 1):
            total = total + self.r_1[r].astype(F32)
        self.part[0] = total
        self.s_2[...] = total.astype(self.dt)
        self.w3 = []
        for r in self.far_first(self.n2):
            to = self.to2(r)
            self.w3.append(self.send(self.s_2.at[to], self.r_2.at[r - 1], self.at2(to)))

    def s4(self):
        for w in self.w3:
            w.wait_recv()
        total = self.part[0, self.i2]
        for r in range(self.n2 - 1):
            total = total + self.r_2[r].astype(F32)
        mine = self.full.at[self.c, self.i1, self.i2]
        self.full[self.c, self.i1, self.i2] = (total * self.scale).astype(self.dt)
        self.w4 = [
            self.send(mine, mine, self.at2(self.to2(r))) for r in self.far_first(self.n2)
        ]

    def s5(self):
        for w in self.w4:
            w.wait_recv()
        mine = self.full.at[self.c, self.i1]
        self.w5 = [
            (r, self.send(mine, mine, self.at1(self.to1(r)))) for r in self.far_first(self.n1)
        ]
        self.w6 = [self.send(mine, mine, self.core)]

    def s6(self):
        for r, w in self.w5[::-1]:
            w.wait_recv()
            piece = self.full.at[self.c, lax.rem(self.i1 + self.n1 - r, self.n1)]
            self.w6.append(self.send(piece, piece, self.core))

    def s7(self):
        for w in self.w6:
            w.wait_recv()


def column(value):
    return jnp.sum(value, axis=1, keepdims=True)


def start_rows(lens_ref, first_row):
    lens = jnp.broadcast_to(lens_ref[...].astype(F32), (128, 128))
    down = lax.broadcasted_iota(jnp.int32, (128, 128), 0)
    across = lax.broadcasted_iota(jnp.int32, (128, 128), 1)
    as_column = column(jnp.where(down == across, lens, 0.0))
    starts = jnp.sum(jnp.where(down < across, as_column, 0.0), axis=0, keepdims=True)
    rows = (first_row + lax.broadcasted_iota(jnp.int32, (ROWS, 128), 0)).astype(F32)
    own = jnp.max(jnp.where(starts <= rows, starts, 0.0), axis=1, keepdims=True)
    return own - first_row.astype(F32)


def kernel(
    tok_h, len_h, win_h, wout_h, gout_h,
    lo, gt, gwin, gwout,
    lens, win, wout,
    xg, gg, wc, xh, xn, xnt, xnp, xr, proj, slope, slope_p, kv, srow,
    w_own, w_prev, sl_own, sl_prev, ds_own, ds_prev,
    stat, gat, att, ee, dgate, datt, dq, dk, dv, dkv_s, dkv_r,
    din, din_s, din_r, stat2, dhid, dh_uq, dh_vk,
    *rest,
):
    reduce_refs, (load_sem, send_sem, recv_sem) = rest[:-3], rest[-3:]
    d, y = lax.axis_index("dp"), lax.axis_index("sub")
    c = lax.rem(d, NC)
    z = lax.rem(d // NC, NZ)
    x = d // (NC * NZ)
    ndp = NX * NZ * NC

    def at(ax, az, ac):
        return ((ax * NZ + az) * NC + ac, y)

    above = (lax.rem(d + 1, ndp), y)
    below = (lax.rem(d + ndp - 1, ndp), y)
    y_peers = [(r, lax.rem(y + r, NY)) for r in (2, 1, 3)]
    y_up, y_down = lax.rem(y + 1, NY), lax.rem(y + NY - 1, NY)

    loads = [
        pltpu.make_async_copy(src, dst, load_sem.at[i])
        for i, (src, dst) in enumerate(
            [
                (tok_h, xg.at[y]), (gout_h, gg.at[y]), (len_h, lens),
                (win_h, win), (wout_h, wout),
            ]
        )
    ]
    for load in loads:
        load.start()

    barrier = pltpu.get_barrier_semaphore()
    greet = [(d, peer) for _, peer in y_peers]
    greet += [at(lax.rem(x + r, NX), z, c) for r in range(1, NX)]
    greet += [at(x, lax.rem(z + r, NZ), c) for r in range(1, NZ)]
    greet += [at(x, z, 1 - c)]
    greet += [(lax.rem(d + ndp + 2 * c - 1, ndp), y)]
    for device in greet:
        pl.semaphore_signal(barrier, inc=1, device_id=device, device_id_type=MESH)
    loads[0].wait()
    loads[1].wait()
    pl.semaphore_wait(barrier, len(greet))

    send = Sender(send_sem, recv_sem)
    core = (c, at(x, z, 1 - c))
    along_x = (NX, x, lambda to: at(to, z, c))
    along_z = (NZ, z, lambda to: at(x, to, c))
    scaling = 1.0 / math.sqrt(ROWS * ndp)
    r_out = Reduce(send, core, along_x, along_z, reduce_refs[0:8], scaling)
    r_uq = Reduce(send, core, along_x, along_z, reduce_refs[8:16], scaling)
    r_vk = Reduce(send, core, along_z, along_x, reduce_refs[16:24], scaling)
    tiles = [slice(t * TILE, (t + 1) * TILE) for t in range(ROWS // TILE)]

    got_x = [
        [send(xg.at[y, rows], xg.at[y, rows], (d, peer)) for _, peer in y_peers]
        for rows in tiles
    ]
    low, high = slice(0, ROWS // 2), slice(ROWS // 2, ROWS)
    pass_up = send(gg.at[y, low], gg.at[y, low], (d, y_up))
    pass_down = send(gg.at[y, high], gg.at[y, high], (d, y_down))
    got_g = [
        send(gg.at[y, high], gg.at[y, high], (d, y_up)),
        send(gg.at[y, low], gg.at[y, low], (d, y_down)),
    ]
    for load in loads[2:]:
        load.wait()
    srow[...] = jnp.broadcast_to(
        start_rows(lens, d * ROWS).astype(jnp.int32), (ROWS, 128)
    )
    wc[y] = wout[:, pl.ds(pl.multiple_of(y * HEAD, HEAD), HEAD)]
    root = 1.0 / math.sqrt(HEAD)

    def attend(scores, begin, width, first, causal):
        scores = scores * root
        col = lax.broadcasted_iota(jnp.int32, scores.shape, 1) + first
        allowed = col >= begin
        if causal is not None:
            row = lax.broadcasted_iota(jnp.int32, scores.shape, 0) + causal
            allowed = allowed & (col <= row)
        sig = 0.5 * jnp.tanh(0.5 * scores) + 0.5
        weight = jnp.where(allowed, scores * sig, 0.0).astype(BF)
        tangent = jnp.where(allowed, sig * (1.0 + scores * (1.0 - sig)) * root, 0.0)
        return weight, tangent

    got_kv = []
    for t, rows in enumerate(tiles):
        for w in got_x[t]:
            w.wait_recv()
        parts = [xg[b, rows].astype(F32) for b in range(NY)]
        mean = column(parts[0] + parts[1] + parts[2] + parts[3]) * (1.0 / WIDTH)
        parts = [part - mean for part in parts]
        var = column(sum(part * part for part in parts)) * (1.0 / WIDTH)
        inv = lax.rsqrt(var + EPSILON)
        xr[rows, :] = jnp.broadcast_to(inv, (TILE, 128))
        for b in range(NY):
            hat = parts[b] * inv
            xh[b, rows] = hat
            xn[rows, b * HEAD : (b + 1) * HEAD] = hat.astype(BF)
        hidden = mm(xn[rows, :], win[...])
        sig = 0.5 * jnp.tanh(0.5 * hidden) + 0.5
        projected = (hidden * sig).astype(BF)
        slopes = sig * (1.0 + hidden * (1.0 - sig))
        for i, g in enumerate((0, 2, 1, 3)):
            cols = slice(g * HEAD, (g + 1) * HEAD)
            proj[i, rows] = projected[:, cols]
            slope[i, rows] = slopes[:, cols]
        got_kv.append(send(proj.at[2:4, rows], kv.at[:, rows], above))
        n = (t + 1) * TILE
        weight, tangent = attend(
            mm(proj[1, rows], proj[3, :n], NT), srow[rows, 0:1], n, 0, t * TILE
        )
        w_own[rows, :n] = weight
        sl_own[rows, :n] = tangent
        att[rows, :] = mm(weight, proj[2, :n])
    got_xn = [send(xn.at[rows], xnp.at[rows], above) for rows in tiles]

    pass_up.wait_recv()
    slot = gg.at[y_down, low]
    got_g.append(send(slot, slot, (d, y_up)))
    pass_down.wait_recv()
    slot = gg.at[y_up, high]
    got_g.append(send(slot, slot, (d, y_down)))
    xnt[:, :ROWS] = xn[...].T

    for t, rows in enumerate(tiles):
        got_kv[t].wait_recv()
        weight, tangent = attend(
            mm(proj[1], kv[1, rows], NT), srow[...], TILE, t * TILE - ROWS, None
        )
        w_prev[:, rows] = weight
        sl_prev[:, rows] = tangent
        att[...] = att[...] + mm(weight, kv[0, rows])

    for w in got_g:
        w.wait_recv()
    d_gated = sum(
        mm(gg[b], wout[:, b * HEAD : (b + 1) * HEAD], NT) for b in range(NY)
    )
    dgate[...] = d_gated
    e = d_gated * proj[0].astype(F32)
    ee[...] = e

    a = att[...]
    sum_a = column(a)
    ca = a - sum_a * (1.0 / HEAD)
    lane = lax.broadcasted_iota(jnp.int32, (ROWS, 128), 1)
    packed = jnp.where(
        lane == 0, sum_a,
        jnp.where(lane == 1, column(ca * ca),
                  jnp.where(lane == 2, column(e), jnp.where(lane == 3, column(e * ca), 0.0))),
    )
    stat[y] = packed.T[:8]
    got_s = [send(stat.at[y], stat.at[y], (d, peer)) for _, peer in y_peers]
    got_w = [
        send(
            wout.at[:, pl.ds(pl.multiple_of(peer * HEAD, HEAD), HEAD)],
            wc.at[y],
            (d, peer),
        )
        for _, peer in y_peers
    ]

    def block_before(t):
        rows = tiles[t]
        got_xn[t].wait_recv()
        for i, g in enumerate((1, 3)):
            hidden = mm(xnp[rows, :], win[:, g * HEAD : (g + 1) * HEAD])
            sig = 0.5 * jnp.tanh(0.5 * hidden) + 0.5
            slope_p[i, rows] = sig * (1.0 + hidden * (1.0 - sig))
        xnt[:, ROWS + t * TILE : ROWS + (t + 1) * TILE] = xnp[rows, :].T

    block_before(0)
    block_before(1)
    for w in got_s:
        w.wait_recv()
    heads = [stat[h] for h in range(NY)]
    mean = sum(h[0:1] for h in heads) * (1.0 / WIDTH)
    var, s_e, s_en = 0.0, 0.0, 0.0
    for h in heads:
        off = h[0:1] * (1.0 / HEAD) - mean
        var = var + h[1:2] + HEAD * off * off
        s_e = s_e + h[2:3]
        s_en = s_en + h[3:4] + off * h[2:3]
    inv = lax.rsqrt(var * (1.0 / WIDTH) + EPSILON)
    line = lax.broadcasted_iota(jnp.int32, (128, ROWS), 0)
    back = jnp.where(
        line == 0, mean,
        jnp.where(line == 1, inv,
                  jnp.where(line == 2, s_e * (1.0 / WIDTH),
                            jnp.where(line == 3, s_en * inv * (1.0 / WIDTH), 0.0))),
    ).T
    mean, inv, s_e, s_en = [back[:, i : i + 1] for i in range(4)]
    normed = (att[...] - mean) * inv
    datt[...] = (inv * (ee[...] - s_e - normed * s_en)).astype(BF)
    gat[y] = (normed * proj[0].astype(F32)).astype(BF)
    dh_uq[0] = (dgate[...] * normed * slope[0]).astype(BF)

    for rows in tiles:
        ds = (mm(datt[rows], kv[0], NT) * sl_prev[rows, :]).astype(BF)
        ds_prev[rows, :] = ds
        dq[rows, :] = mm(ds, kv[1])
    back_v = mm(w_prev[...], datt[...], TN)
    dkv_s[0] = back_v.astype(BF)
    got_dv = send(dkv_s.at[0], dkv_r.at[0], below)
    back_k = mm(ds_prev[...], proj[1], TN)
    dkv_s[1] = back_k.astype(BF)
    got_dk = send(dkv_s.at[1], dkv_r.at[1], below)
    block_before(2)
    block_before(3)
    dh_vk[0, ROWS:] = (back_v * slope_p[0]).astype(BF)
    dh_vk[1, ROWS:] = (back_k * slope_p[1]).astype(BF)
    got_a = [send(gat.at[y], gat.at[y], (d, peer)) for _, peer in y_peers]

    for t, rows in enumerate(tiles):
        n = (t + 1) * TILE
        ds = (mm(datt[rows], proj[2, :n], NT) * sl_own[rows, :n]).astype(BF)
        ds_own[rows, :n] = ds
        dq[rows, :] = dq[rows, :] + mm(ds, proj[3, :n])
    for t, cols in enumerate(tiles):
        dk[cols, :] = mm(ds_own[t * TILE :, cols], proj[1, t * TILE :], TN)
        dv[cols, :] = mm(w_own[t * TILE :, cols], datt[t * TILE :], TN)

    dh_vk[0, :ROWS] = (dv[...] * slope[2]).astype(BF)
    dh_vk[1, :ROWS] = (dk[...] * slope[3]).astype(BF)
    r_vk.s1(mm(xnt[...], dh_vk[1 - c]))
    dh_uq[1] = (dq[...] * slope[1]).astype(BF)
    r_uq.s1(mm(xnt[:, :ROWS], dh_uq[1 - c]))
    gated_t = gat[y].T
    r_out.s1(jnp.concatenate([mm(gated_t, gg[2 * (1 - c) + i]) for i in range(2)], 0))
    r_vk.keep(mm(xnt[...], dh_vk[c]))
    r_vk.s2()
    r_uq.keep(mm(xnt[:, :ROWS], dh_uq[c]))
    r_uq.s2()
    r_out.keep(jnp.concatenate([mm(gated_t, gg[2 * c + i]) for i in range(2)], 0))
    r_out.s2()

    dhid[:, 0:HEAD] = dh_uq[0]
    dhid[:, 2 * HEAD : 3 * HEAD] = dh_uq[1]
    got_dv.wait_recv()
    dhid[:, HEAD : 2 * HEAD] = ((dv[...] + dkv_r[0].astype(F32)) * slope[2]).astype(BF)
    got_dk.wait_recv()
    dhid[:, 3 * HEAD :] = ((dk[...] + dkv_r[1].astype(F32)) * slope[3]).astype(BF)
    one, two = 0.0, 0.0
    for b in range(NY):
        part = mm(dhid[...], win[b * HEAD : (b + 1) * HEAD, :], NT)
        one = one + part
        two = two + part * xh[b]
        din[b] = part
        din_s[b] = part.astype(BF)
    packed = jnp.where(lane == 0, column(one), jnp.where(lane == 1, column(two), 0.0))
    stat2[y] = packed.T[:8]
    got_i = [send(din_s.at[peer], din_r.at[r - 1], (d, peer)) for r, peer in y_peers]
    got_t = [send(stat2.at[y], stat2.at[y], (d, peer)) for _, peer in y_peers]
    r_uq.s3()
    r_vk.s3()
    r_out.s3()

    for w in got_a + got_w:
        w.wait_recv()
    lo[...] = (
        xg[y].astype(F32) + sum(mm(gat[h], wc[h]) for h in range(NY))
    ).astype(BF)

    r_vk.s4()
    r_uq.s4()
    r_out.s4()
    r_vk.s5()
    r_uq.s5()
    r_out.s5()

    for w in got_i + got_t:
        w.wait_recv()
    total = din[y]
    for r in range(NY - 1):
        total = total + din_r[r].astype(F32)
    both = (stat2[0] + stat2[1] + stat2[2] + stat2[3]) * (1.0 / WIDTH)
    back = jnp.where(line == 0, both[0:1], jnp.where(line == 1, both[1:2], 0.0)).T
    piece = xr[:, 0:1] * (total - back[:, 0:1] - xh[y] * back[:, 1:2])
    gt[...] = (gg[y].astype(F32) + piece).astype(BF)

    r_uq.s6()
    r_out.s6()
    r_vk.s6()
    r_uq.s7()
    for i, g in enumerate((0, 2)):
        gwin[:, g * HEAD : (g + 1) * HEAD] = r_uq.full[i].reshape(ROWS, HEAD).astype(F32)
    r_out.s7()
    for b in range(NY):
        block = r_out.full[b // 2, (b % 2) * 2 : (b % 2) * 2 + 2]
        gwout[:, b * HEAD : (b + 1) * HEAD] = block.reshape(HEAD, HEAD)
    r_vk.s7()
    for i, g in enumerate((1, 3)):
        gwin[:, g * HEAD : (g + 1) * HEAD] = r_vk.full[i].reshape(ROWS, HEAD).astype(F32)
    for w in send.copies:
        w.wait_send()


def store(*refs):
    sources, targets, sem = refs[:4], refs[4:8], refs[8]
    copies = [
        pltpu.make_async_copy(src, dst, sem.at[i])
        for i, (src, dst) in enumerate(zip(sources, targets))
    ]
    for copy in copies:
        copy.start()
    for copy in copies:
        copy.wait()


def reduce_scratch(n1, n2, rows, dt):
    block = (n1, n2, rows, HEAD)
    return [
        pltpu.VMEM(block, F32),
        pltpu.VMEM(block, dt),
        pltpu.VMEM(block, dt),
        pltpu.VMEM(block, dt),
        pltpu.VMEM((n1 - 1, n2, rows, HEAD), dt),
        pltpu.VMEM((n2, rows, HEAD), dt),
        pltpu.VMEM((n2 - 1, rows, HEAD), dt),
        pltpu.VMEM((NC,) + block, dt),
    ]


def shards(tokens, lengths, weight_in, weight_out, grad_out):
    lengths = lengths.reshape(1, -1)
    vm = pl.BlockSpec(memory_space=pltpu.VMEM)
    hbm = pl.BlockSpec(memory_space=pltpu.HBM)
    blocks = lambda n, dt: pltpu.VMEM((n, ROWS, HEAD), dt)
    full = lambda dt: pltpu.VMEM((ROWS, WIDTH), dt)
    one = lambda dt: pltpu.VMEM((ROWS, HEAD), dt)
    stats = pltpu.VMEM((NY, 8, ROWS), F32)
    scratch = [
        pltpu.VMEM((1, 128), jnp.int32), full(BF), pltpu.VMEM((HEAD, WIDTH), BF),
        blocks(NY, BF), blocks(NY, BF), pltpu.VMEM((NY, HEAD, HEAD), BF),
        blocks(NY, F32), full(BF), pltpu.VMEM((WIDTH, 2 * ROWS), BF), full(BF), one(F32),
        blocks(4, BF), blocks(4, F32), blocks(2, F32), blocks(2, BF), one(jnp.int32),
        full(BF), full(BF), full(F32), full(F32), full(BF), full(BF),
        stats, blocks(NY, BF), one(F32), one(F32), one(F32), one(BF),
        one(F32), one(F32), one(F32), blocks(2, BF), blocks(2, BF),
        blocks(NY, F32), blocks(NY, BF), blocks(NY - 1, BF), stats,
        full(BF), blocks(2, BF), pltpu.VMEM((2, 2 * ROWS, HEAD), BF),
        *reduce_scratch(NX, NZ, 8, F32),
        *reduce_scratch(NX, NZ, 16, BF),
        *reduce_scratch(NZ, NX, 16, BF),
        pltpu.SemaphoreType.DMA((5,)),
        pltpu.SemaphoreType.DMA((160,)),
        pltpu.SemaphoreType.DMA((160,)),
    ]
    shapes = (
        jax.ShapeDtypeStruct((ROWS, HEAD), BF),
        jax.ShapeDtypeStruct((ROWS, HEAD), BF),
        jax.ShapeDtypeStruct((WIDTH, 4 * HEAD), F32),
        jax.ShapeDtypeStruct((HEAD, WIDTH), F32),
    )
    results = pl.pallas_call(
        kernel,
        out_shape=shapes,
        in_specs=[hbm] * 5,
        out_specs=(vm,) * 4,
        scratch_shapes=scratch,
        compiler_params=pltpu.CompilerParams(
            collective_id=0, has_side_effects=True, vmem_limit_bytes=62 * 1024 * 1024
        ),
        name="layer",
    )(tokens, lengths, weight_in, weight_out, grad_out)
    return pl.pallas_call(
        store,
        out_shape=shapes,
        in_specs=[vm] * 4,
        out_specs=(hbm,) * 4,
        scratch_shapes=[pltpu.SemaphoreType.DMA((4,))],
        name="store",
    )(*results)


def solution(mesh):
    placed = (P("dp", "sub"), P(), P(None, "sub"), P("sub", None), P("dp", "sub"))
    return jax.shard_map(
        shards,
        mesh=mesh,
        in_specs=placed,
        out_specs=(P("dp", "sub"), P("dp", "sub"), P(None, "sub"), P("sub", None)),
        check_vma=False,
    )
```

time: 69.6 us -> 61.1 us (0.88)
  local copies, waits for them, and re-layouts: 7.38 us -> 0 us
  Pallas kernels: 61.3 us -> 60.3 us
    unnamed x14 -> x0, local copies, waits for them, and re-layouts: 7.38 us -> none
    pallas_call x1 -> x2, Pallas kernels: 61.3 us -> 60.3 us  [the longest x1 57.7 us: shards(): pl.pallas_call(kernel, out_shape=shapes, in_specs=[hbm] * 5, out_specs=(v...]
where the time goes in v2:
time: 61.1 us; the launch traced here: 60.9 us
  Pallas kernels  60.3 us (99%)
  between operations  0.64 us (1%)
    pallas_call x1, Pallas kernels, shards(): pl.pallas_call(kernel, out_shape=shapes, in_specs=[hbm] * 5, out_specs=(v...  57.7 us
    pallas_call x1, Pallas kernels, shards(): pl.pallas_call(store, out_shape=shapes, in_specs=[vm] * 4, out_specs=(hbm...  2.57 us

profile of v2, /device:TPU:1, one launch (start us, length us, event | category | flops | bytes accessed | tf_op | source)
XLA Modules:
  0.0 60.9 jit_solution(17011500911659818722)
XLA Ops:
  0.6 57.7 %layer.1 = (bf16[512,128]{1,0:T(8,128)(2,1)}, bf16[512,128]{1,0:T(8,128)(2,1)}, f32[512,512]{1,0:T(8,128)}, f32[128,512]{1,0:T(8,128)}) custom-call(bf16[512,128]{1,0:T(8,128)(2,1)} %tok_h.1, s32[1,128]{1,0:T(1,128)} %bitcast.1, bf16[512,512]{1,0:T(8,128)(2,1)} %win_h.1, bf16[128,512]{1,0:T(8,128)(2,1)} %wout_h.1, bf16[512,128]{1,0:T(8,128)(2,1)} %gout_h.1), custom_call_target="tpu_custom_call" | custom-call | tf_op jit(solution)/shard_map/layer/pallas_call | solution.py:502
  58.4 2.6 %store.1 = (bf16[512,128]{1,0:T(8,128)(2,1)}, bf16[512,128]{1,0:T(8,128)(2,1)}, f32[512,512]{1,0:T(8,128)}, f32[128,512]{1,0:T(8,128)}) custom-call(bf16[512,128]{1,0:T(8,128)(2,1)} %get-tuple-element.8.refs_0_, bf16[512,128]{1,0:T(8,128)(2,1)} %get-tuple-element.9.refs_1_, f32[512,512]{1,0:T(8,128)} %get-tuple-element.10.refs_2_, ...), custom_call_target="tpu_custom_call" | custom-call | tf_op jit(solution)/shard_map/store/pallas_call | solution.py:513

commit v3 on v2

v3 whole, which is shorter than its diff:
```python
import functools
import math

import jax
import jax.numpy as jnp
from jax import lax
from jax.experimental import pallas as pl
from jax.experimental.pallas import tpu as pltpu
from jax.sharding import PartitionSpec as P

EPSILON = 1e-05
NX, NZ, NC, NY = 4, 8, 2, 4
ROWS, HEAD, WIDTH = 512, 128, 512
TILE = 128
MESH = pl.DeviceIdType.MESH
BF, F32 = jnp.bfloat16, jnp.float32

NN = (((1,), (0,)), ((), ()))
NT = (((1,), (1,)), ((), ()))
TN = (((0,), (0,)), ((), ()))


def mm(left, right, dims=NN):
    return lax.dot_general(left, right, dims, preferred_element_type=F32)


class Copy:
    def __init__(self, copy):
        self.copy, self.left, self.landed = copy, False, False
        copy.start()

    def wait_recv(self):
        if not self.landed:
            self.copy.wait_recv()
        self.landed = True

    def wait_send(self):
        if not self.left:
            self.copy.wait_send()
        self.left = True


class Sender:
    def __init__(self, send_sem, recv_sem):
        self.send_sem, self.recv_sem, self.copies = send_sem, recv_sem, []

    def __call__(self, src, dst, device):
        i = len(self.copies)
        copy = Copy(
            pltpu.make_async_remote_copy(
                src_ref=src,
                dst_ref=dst,
                send_sem=self.send_sem.at[i],
                recv_sem=self.recv_sem.at[i],
                device_id=device,
                device_id_type=MESH,
            )
        )
        self.copies.append(copy)
        return copy


def far_first(n):
    return sorted(range(1, n), key=lambda r: (-min(r, n - r), r))


class Reduce:
    def __init__(self, send, core, first, second, refs, scale):
        self.send, self.scale = send, scale
        self.c, self.core = core
        self.n1, self.i1, self.at1 = first
        self.n2, self.i2, self.at2 = second
        self.part, self.sb, self.rc, self.s_1, self.r_1, self.s_2, self.r_2, self.full = refs
        self.dt = self.full.dtype

    def to1(self, r):
        return lax.rem(self.i1 + r, self.n1)

    def to2(self, r):
        return lax.rem(self.i2 + r, self.n2)

    def s1(self, other):
        self.sb[...] = other.astype(self.dt).reshape(self.sb.shape)
        self.w1 = self.send(self.sb, self.rc, self.core)

    def keep(self, own):
        self.part[...] = own.reshape(self.part.shape)

    def s2(self):
        self.w1.wait_recv()
        total = self.part[...] + self.rc[...].astype(F32)
        self.part[...] = total
        self.s_1[...] = total.astype(self.dt)
        self.w2 = []
        for r in far_first(self.n1):
            to = self.to1(r)
            self.w2.append(self.send(self.s_1.at[to], self.r_1.at[r - 1], self.at1(to)))

    def s3(self):
        for w in self.w2:
            w.wait_recv()
        total = self.part[self.i1]
        for r in range(self.n1 - 1):
            total = total + self.r_1[r].astype(F32)
        self.part[0] = total
        self.s_2[...] = total.astype(self.dt)
        self.w3 = []
        for r in far_first(self.n2):
            to = self.to2(r)
            self.w3.append(self.send(self.s_2.at[to], self.r_2.at[r - 1], self.at2(to)))

    def s4(self):
        for w in self.w3:
            w.wait_recv()
        total = self.part[0, self.i2]
        for r in range(self.n2 - 1):
            total = total + self.r_2[r].astype(F32)
        mine = self.full.at[self.c, self.i1, self.i2]
        self.full[self.c, self.i1, self.i2] = (total * self.scale).astype(self.dt)
        self.w4 = [
            self.send(mine, mine, self.at2(self.to2(r))) for r in far_first(self.n2)
        ]

    def s5(self):
        for w in self.w4:
            w.wait_recv()
        mine = self.full.at[self.c, self.i1]
        self.w5 = [
            (r, self.send(mine, mine, self.at1(self.to1(r)))) for r in far_first(self.n1)
        ]
        self.w6 = [self.send(mine, mine, self.core)]

    def s6(self):
        for r, w in self.w5[::-1]:
            w.wait_recv()
            piece = self.full.at[self.c, lax.rem(self.i1 + self.n1 - r, self.n1)]
            self.w6.append(self.send(piece, piece, self.core))

    def s7(self):
        for w in self.w6:
            w.wait_recv()


class Reduce3:
    def __init__(self, send, core, first, second, refs, scale):
        self.send, self.scale = send, scale
        self.c, self.core = core
        self.n1, self.i1, self.at1 = first
        self.n2, self.i2, self.at2 = second
        self.part, self.sb, self.rc, self.s_1, self.r_1, self.both, self.full = refs
        self.dt = self.full.dtype

    def s1(self, other):
        self.sb[...] = other.astype(self.dt).reshape(self.sb.shape)
        self.w1 = self.send(self.sb, self.rc, self.core)

    def keep(self, own):
        self.part[...] = own.reshape(self.part.shape)

    def s2(self):
        self.w1.wait_recv()
        total = self.part[...] + self.rc[...].astype(F32)
        self.part[...] = total
        self.s_1[...] = total.astype(self.dt)
        self.w2 = []
        for r in far_first(self.n1):
            to = lax.rem(self.i1 + r, self.n1)
            self.w2.append(self.send(self.s_1.at[to], self.r_1.at[r - 1], self.at1(to)))

    def s3(self):
        for w in self.w2:
            w.wait_recv()
        total = self.part[self.i1]
        for r in range(self.n1 - 1):
            total = total + self.r_1[r].astype(F32)
        self.both[self.i2] = total.astype(self.dt)
        mine = self.both.at[self.i2]
        self.w3 = [
            self.send(mine, mine, self.at2(lax.rem(self.i2 + r, self.n2)))
            for r in far_first(self.n2)
        ]

    def s4(self):
        for w in self.w3:
            w.wait_recv()
        total = self.both[0].astype(F32)
        for k in range(1, self.n2):
            total = total + self.both[k].astype(F32)
        self.full[self.c, self.i1] = (total * self.scale).astype(self.dt)
        mine = self.full.at[self.c, self.i1]
        self.w4 = [
            (r, self.send(mine, mine, self.at1(lax.rem(self.i1 + r, self.n1))))
            for r in far_first(self.n1)
        ]
        self.w5 = [self.send(mine, mine, self.core)]

    def s5(self):
        for r, w in self.w4[::-1]:
            w.wait_recv()
            piece = self.full.at[self.c, lax.rem(self.i1 + self.n1 - r, self.n1)]
            self.w5.append(self.send(piece, piece, self.core))

    def s6(self):
        for w in self.w5:
            w.wait_recv()


def column(value):
    return jnp.sum(value, axis=1, keepdims=True)


def start_rows(lens_ref, first_row):
    lens = jnp.broadcast_to(lens_ref[...].astype(F32), (128, 128))
    down = lax.broadcasted_iota(jnp.int32, (128, 128), 0)
    across = lax.broadcasted_iota(jnp.int32, (128, 128), 1)
    as_column = column(jnp.where(down == across, lens, 0.0))
    starts = jnp.sum(jnp.where(down < across, as_column, 0.0), axis=0, keepdims=True)
    rows = (first_row + lax.broadcasted_iota(jnp.int32, (ROWS, 128), 0)).astype(F32)
    own = jnp.max(jnp.where(starts <= rows, starts, 0.0), axis=1, keepdims=True)
    return own - first_row.astype(F32)


def kernel(
    tok_h, len_h, win_h, wout_h, gout_h,
    lo, gt, gwin, gwout,
    lens, win, wout, lo_v, gt_v, gwin_v, gwout_v,
    xg, gg, wc, xh, xn, xnt, xnp, xr, gate, qb, kv, slope, slope_p, srow,
    wt, sl, slt, wp,
    stat, gat, att, ee, dgate, datt, ds, dk, dv, dkv_s, dkv_r,
    din, din_s, din_r, stat2, dhid, dh_u, dh_q, dh_vk, pair,
    *rest,
):
    reduce_refs, (load_sem, out_sem, send_sem, recv_sem) = rest[:-4], rest[-4:]
    d, y = lax.axis_index("dp"), lax.axis_index("sub")
    c = lax.rem(d, NC)
    z = lax.rem(d // NC, NZ)
    x = d // (NC * NZ)
    ndp = NX * NZ * NC

    def at(ax, az, ac):
        return ((ax * NZ + az) * NC + ac, y)

    above = (lax.rem(d + 1, ndp), y)
    below = (lax.rem(d + ndp - 1, ndp), y)
    y_peers = [(r, lax.rem(y + r, NY)) for r in (2, 1, 3)]
    y_up, y_down = lax.rem(y + 1, NY), lax.rem(y + NY - 1, NY)

    loads = [
        pltpu.make_async_copy(src, dst, load_sem.at[i])
        for i, (src, dst) in enumerate(
            [
                (tok_h, xg.at[y]), (gout_h, gg.at[y]), (len_h, lens),
                (win_h, win), (wout_h, wout),
            ]
        )
    ]
    for load in loads:
        load.start()
    stores = []

    def put(src, dst):
        copy = pltpu.make_async_copy(src, dst, out_sem.at[len(stores)])
        copy.start()
        stores.append(copy)

    barrier = pltpu.get_barrier_semaphore()
    greet = [(d, peer) for _, peer in y_peers]
    greet += [at(lax.rem(x + r, NX), z, c) for r in range(1, NX)]
    greet += [at(x, lax.rem(z + r, NZ), c) for r in range(1, NZ)]
    greet += [at(x, z, 1 - c)]
    greet += [(lax.rem(d + ndp + 2 * c - 1, ndp), y)]
    for device in greet:
        pl.semaphore_signal(barrier, inc=1, device_id=device, device_id_type=MESH)
    for load in loads:
        load.wait()
    pl.semaphore_wait(barrier, len(greet))

    send = Sender(send_sem, recv_sem)
    core = (c, at(x, z, 1 - c))
    along_x = (NX, x, lambda to: at(to, z, c))
    along_z = (NZ, z, lambda to: at(x, to, c))
    scaling = 1.0 / math.sqrt(ROWS * ndp)
    r_uo = Reduce(send, core, along_x, along_z, reduce_refs[0:8], scaling)
    r_vk = Reduce3(send, core, along_z, along_x, reduce_refs[8:15], scaling)
    r_q = Reduce3(send, core, along_z, along_x, reduce_refs[15:22], scaling)
    tiles = [slice(t * TILE, (t + 1) * TILE) for t in range(ROWS // TILE)]
    half = ROWS // 2
    low, high = slice(0, half), slice(half, ROWS)

    got_x = []
    for rows in tiles:
        got_x.append([send(xg.at[y, rows], xg.at[y, rows], (d, peer)) for _, peer in y_peers])
    pass_up = send(gg.at[y, low], gg.at[y, low], (d, y_up))
    pass_down = send(gg.at[y, high], gg.at[y, high], (d, y_down))
    got_g = [
        send(gg.at[y, high], gg.at[y, high], (d, y_up)),
        send(gg.at[y, low], gg.at[y, low], (d, y_down)),
    ]
    srow[...] = jnp.broadcast_to(
        start_rows(lens, d * ROWS).astype(jnp.int32), (ROWS, 128)
    )
    wc[y] = wout[:, pl.ds(pl.multiple_of(y * HEAD, HEAD), HEAD)]
    root = 1.0 / math.sqrt(HEAD)

    def attend(scores, begin, first, causal):
        scores = scores * root
        col = lax.broadcasted_iota(jnp.int32, scores.shape, 1) + first
        allowed = col >= begin
        if causal is not None:
            row = lax.broadcasted_iota(jnp.int32, scores.shape, 0) + causal
            allowed = allowed & (col <= row)
        sig = 0.5 * jnp.tanh(0.5 * scores) + 0.5
        weight = jnp.where(allowed, scores * sig, 0.0).astype(BF)
        tangent = jnp.where(allowed, sig * (1.0 + scores * (1.0 - sig)) * root, 0.0)
        return weight, tangent

    got_kv = []
    for t, rows in enumerate(tiles):
        for w in got_x[t]:
            w.wait_recv()
        parts = [xg[b, rows].astype(F32) for b in range(NY)]
        mean = column(parts[0] + parts[1] + parts[2] + parts[3]) * (1.0 / WIDTH)
        parts = [part - mean for part in parts]
        var = column(sum(part * part for part in parts)) * (1.0 / WIDTH)
        inv = lax.rsqrt(var + EPSILON)
        xr[rows, :] = jnp.broadcast_to(inv, (TILE, 128))
        for b in range(NY):
            hat = parts[b] * inv
            xh[b, rows] = hat
            xn[rows, b * HEAD : (b + 1) * HEAD] = hat.astype(BF)
        hidden = mm(xn[rows, :], win[...])
        sig = 0.5 * jnp.tanh(0.5 * hidden) + 0.5
        projected = (hidden * sig).astype(BF)
        own = slice(ROWS + t * TILE, ROWS + (t + 1) * TILE)
        kv[0, own] = projected[:, HEAD : 2 * HEAD]
        kv[1, own] = projected[:, 3 * HEAD :]
        got_kv.append(send(kv.at[:, own], kv.at[:, rows], above))
        gate[rows, :] = projected[:, :HEAD]
        qb[rows, :] = projected[:, 2 * HEAD : 3 * HEAD]
        slopes = sig * (1.0 + hidden * (1.0 - sig))
        for i, g in enumerate((0, 2, 1, 3)):
            slope[i, rows] = slopes[:, g * HEAD : (g + 1) * HEAD]

    pass_up.wait_recv()
    slot = gg.at[y_down, low]
    got_g.append(send(slot, slot, (d, y_up)))
    pass_down.wait_recv()
    slot = gg.at[y_up, high]
    got_g.append(send(slot, slot, (d, y_down)))

    for t, rows in enumerate(tiles):
        weight, tangent = attend(
            mm(qb[rows, :], kv[1, ROWS:], NT), srow[rows, 0:1], 0, t * TILE
        )
        wt[ROWS:, rows] = weight.T
        sl[rows, ROWS:] = tangent
        slt[ROWS:, rows] = tangent.T
        att[rows, :] = mm(weight, kv[0, ROWS:])
    got_xn = [send(xn.at[rows], xnp.at[rows], above) for rows in (low, high)]
    xnt[:, ROWS:] = xn[...].T

    for t, cols in enumerate(tiles):
        got_kv[t].wait_recv()
        weight, tangent = attend(
            mm(qb[...], kv[1, cols], NT), srow[...], t * TILE - ROWS, None
        )
        wp[:, cols] = weight
        sl[:, cols] = tangent
        att[...] = att[...] + mm(weight, kv[0, cols])

    for w in got_g:
        w.wait_recv()
    d_gated = sum(
        mm(gg[b], wout[:, b * HEAD : (b + 1) * HEAD], NT) for b in range(NY)
    )
    dgate[...] = d_gated
    e = d_gated * gate[...].astype(F32)
    ee[...] = e

    a = att[...]
    sum_a = column(a)
    ca = a - sum_a * (1.0 / HEAD)
    lane = lax.broadcasted_iota(jnp.int32, (ROWS, 128), 1)
    packed = jnp.where(
        lane == 0, sum_a,
        jnp.where(lane == 1, column(ca * ca),
                  jnp.where(lane == 2, column(e), jnp.where(lane == 3, column(e * ca), 0.0))),
    )
    stat[y] = packed.T[:8]
    got_s = [send(stat.at[y], stat.at[y], (d, peer)) for _, peer in y_peers]
    for rows in tiles:
        wt[rows, :] = wp[:, rows].T
        slt[rows, :] = sl[:, rows].T
    for w in got_s:
        w.wait_recv()
    heads = [stat[h] for h in range(NY)]
    mean = sum(h[0:1] for h in heads) * (1.0 / WIDTH)
    var, s_e, s_en = 0.0, 0.0, 0.0
    for h in heads:
        off = h[0:1] * (1.0 / HEAD) - mean
        var = var + h[1:2] + HEAD * off * off
        s_e = s_e + h[2:3]
        s_en = s_en + h[3:4] + off * h[2:3]
    inv = lax.rsqrt(var * (1.0 / WIDTH) + EPSILON)
    line = lax.broadcasted_iota(jnp.int32, (128, ROWS), 0)
    back = jnp.where(
        line == 0, mean,
        jnp.where(line == 1, inv,
                  jnp.where(line == 2, s_e * (1.0 / WIDTH),
                            jnp.where(line == 3, s_en * inv * (1.0 / WIDTH), 0.0))),
    ).T
    mean, inv, s_e, s_en = [back[:, i : i + 1] for i in range(4)]
    normed = (att[...] - mean) * inv
    datt[...] = (inv * (ee[...] - s_e - normed * s_en)).astype(BF)
    gat[y] = (normed * gate[...].astype(F32)).astype(BF)
    got_a = [send(gat.at[y], gat.at[y], (d, peer)) for _, peer in y_peers]
    got_w = [
        send(
            wout.at[:, pl.ds(pl.multiple_of(peer * HEAD, HEAD), HEAD)],
            wc.at[y],
            (d, peer),
        )
        for _, peer in y_peers
    ]
    dh_u[...] = (dgate[...] * normed * slope[0]).astype(BF)

    gated_t = gat[y].T
    pair[0] = mm(xnt[:, ROWS:], dh_u[...])
    for b in range(NY):
        pair[1, b * HEAD : (b + 1) * HEAD] = mm(gated_t, gg[b])
    r_uo.s1(pair[1 - c])
    r_uo.keep(pair[c])

    def key_grads(rows):
        d_st = (mm(kv[0, rows], datt[...], NT) * slt[rows, :]).astype(BF)
        dk[rows, :] = mm(d_st, qb[...])
        dv[rows, :] = mm(wt[rows, :], datt[...])

    for t in range(ROWS // TILE):
        key_grads(tiles[t])
    dkv_s[0] = dv[:ROWS, :].astype(BF)
    dkv_s[1] = dk[:ROWS, :].astype(BF)
    got_dkv = send(dkv_s, dkv_r, below)
    for t in range(ROWS // TILE):
        key_grads(slice(ROWS + t * TILE, ROWS + (t + 1) * TILE))
    r_uo.s2()

    for t, rows in enumerate((low, high)):
        got_xn[t].wait_recv()
        for i, g in enumerate((1, 3)):
            hidden = mm(xnp[rows, :], win[:, g * HEAD : (g + 1) * HEAD])
            sig = 0.5 * jnp.tanh(0.5 * hidden) + 0.5
            slope_p[i, rows] = sig * (1.0 + hidden * (1.0 - sig))
        xnt[:, rows] = xnp[rows, :].T
    dh_vk[:ROWS, :HEAD] = (dv[:ROWS, :] * slope_p[0]).astype(BF)
    dh_vk[:ROWS, HEAD:] = (dk[:ROWS, :] * slope_p[1]).astype(BF)
    dh_vk[ROWS:, :HEAD] = (dv[ROWS:, :] * slope[2]).astype(BF)
    dh_vk[ROWS:, HEAD:] = (dk[ROWS:, :] * slope[3]).astype(BF)
    mine = pl.ds(pl.multiple_of(c * half, half), half)
    theirs = pl.ds(pl.multiple_of((1 - c) * half, half), half)
    r_vk.s1(mm(xnt[theirs, :], dh_vk[...]))

    for rows in tiles:
        ds[rows, :] = (mm(datt[rows, :], kv[0], NT) * sl[rows, :]).astype(BF)
        dq = mm(ds[rows, :], kv[1])
        dh_q[rows, :] = (dq * slope[1, rows]).astype(BF)
    r_q.s1(mm(xnt[theirs, ROWS:], dh_q[...]))
    r_vk.keep(mm(xnt[mine, :], dh_vk[...]))
    r_vk.s2()
    r_q.keep(mm(xnt[mine, ROWS:], dh_q[...]))
    r_q.s2()
    r_uo.s3()

    dhid[:, 0:HEAD] = dh_u[...]
    dhid[:, 2 * HEAD : 3 * HEAD] = dh_q[...]
    got_dkv.wait_recv()
    dhid[:, HEAD : 2 * HEAD] = ((dv[ROWS:, :] + dkv_r[0].astype(F32)) * slope[2]).astype(BF)
    dhid[:, 3 * HEAD :] = ((dk[ROWS:, :] + dkv_r[1].astype(F32)) * slope[3]).astype(BF)
    one, two = 0.0, 0.0
    for b in range(NY):
        part = mm(dhid[...], win[b * HEAD : (b + 1) * HEAD, :], NT)
        one = one + part
        two = two + part * xh[b]
        din[b] = part
        din_s[b] = part.astype(BF)
    packed = jnp.where(lane == 0, column(one), jnp.where(lane == 1, column(two), 0.0))
    stat2[y] = packed.T[:8]
    got_i = [send(din_s.at[peer], din_r.at[r - 1], (d, peer)) for r, peer in y_peers]
    got_t = [send(stat2.at[y], stat2.at[y], (d, peer)) for _, peer in y_peers]
    for w in got_a + got_w:
        w.wait_recv()
    lo_v[...] = (
        xg[y].astype(F32) + sum(mm(gat[h], wc[h]) for h in range(NY))
    ).astype(BF)
    put(lo_v, lo)
    r_vk.s3()
    r_q.s3()
    r_uo.s4()
    r_vk.s4()
    r_q.s4()
    r_uo.s5()

    for w in got_i + got_t:
        w.wait_recv()
    total = din[y]
    for r in range(NY - 1):
        total = total + din_r[r].astype(F32)
    both = (stat2[0] + stat2[1] + stat2[2] + stat2[3]) * (1.0 / WIDTH)
    back = jnp.where(line == 0, both[0:1], jnp.where(line == 1, both[1:2], 0.0)).T
    piece = xr[:, 0:1] * (total - back[:, 0:1] - xh[y] * back[:, 1:2])
    gt_v[...] = (gg[y].astype(F32) + piece).astype(BF)
    put(gt_v, gt)

    def put_columns(g, value):
        cols = slice(g * HEAD, (g + 1) * HEAD)
        gwin_v[:, cols] = value.astype(F32)
        put(gwin_v.at[:, cols], gwin.at[:, cols])

    r_vk.s5()
    r_q.s5()
    r_uo.s6()
    r_vk.s6()
    done = r_vk.full[...].reshape(ROWS, 2 * HEAD)
    put_columns(1, done[:, :HEAD])
    put_columns(3, done[:, HEAD:])
    r_q.s6()
    put_columns(2, r_q.full[...].reshape(ROWS, HEAD))
    r_uo.s7()
    put_columns(0, r_uo.full[0].reshape(ROWS, HEAD))
    for b in range(NY):
        gwout_v[:, b * HEAD : (b + 1) * HEAD] = r_uo.full[1, b].reshape(HEAD, HEAD).astype(F32)
    put(gwout_v, gwout)
    for w in send.copies:
        w.wait_send()
    for w in stores:
        w.wait()


def store(*refs):
    sources, targets, stages, sems = refs[:4], refs[4:8], refs[8:12], refs[12:]
    parts = [(i, slice(None)) for i in (0, 1, 3)]
    parts += [(2, slice(t * TILE, (t + 1) * TILE)) for t in range(WIDTH // TILE)]
    reads, writes = [], []
    for n, (i, rows) in enumerate(parts):
        stage = stages[i].at[rows]
        reads.append(pltpu.make_async_copy(sources[i].at[rows], stage, sems[0].at[n]))
        writes.append(pltpu.make_async_copy(stage, targets[i].at[rows], sems[1].at[n]))
    for read in reads:
        read.start()
    for read, write in zip(reads, writes):
        read.wait()
        write.start()
    for write in writes:
        write.wait()


def reduce3_scratch(n):
    r = ROWS // (NC * NZ)
    block = (NZ, r, n)
    return [
        pltpu.VMEM(block, F32),
        pltpu.VMEM(block, BF),
        pltpu.VMEM(block, BF),
        pltpu.VMEM(block, BF),
        pltpu.VMEM((NZ - 1, r, n), BF),
        pltpu.VMEM((NX, r, n), BF),
        pltpu.VMEM((NC,) + block, BF),
    ]


def reduce_scratch(n1, n2, rows, dt):
    block = (n1, n2, rows, HEAD)
    return [
        pltpu.VMEM(block, F32),
        pltpu.VMEM(block, dt),
        pltpu.VMEM(block, dt),
        pltpu.VMEM(block, dt),
        pltpu.VMEM((n1 - 1, n2, rows, HEAD), dt),
        pltpu.VMEM((n2, rows, HEAD), dt),
        pltpu.VMEM((n2 - 1, rows, HEAD), dt),
        pltpu.VMEM((NC,) + block, dt),
    ]


def shards(tokens, lengths, weight_in, weight_out, grad_out):
    lengths = lengths.reshape(1, -1)
    hbm = pl.BlockSpec(memory_space=pltpu.HBM)
    blocks = lambda n, dt: pltpu.VMEM((n, ROWS, HEAD), dt)
    full = lambda dt: pltpu.VMEM((ROWS, WIDTH), dt)
    one = lambda dt: pltpu.VMEM((ROWS, HEAD), dt)
    tall = lambda n, dt: pltpu.VMEM((2 * ROWS, n), dt)
    stats = pltpu.VMEM((NY, 8, ROWS), F32)
    scratch = [
        pltpu.VMEM((1, 128), jnp.int32), full(BF), pltpu.VMEM((HEAD, WIDTH), BF),
        one(BF), one(BF), full(F32), pltpu.VMEM((HEAD, WIDTH), F32),
        blocks(NY, BF), blocks(NY, BF), pltpu.VMEM((NY, HEAD, HEAD), BF),
        blocks(NY, F32), full(BF), pltpu.VMEM((WIDTH, 2 * ROWS), BF), full(BF), one(F32),
        one(BF), one(BF), pltpu.VMEM((2, 2 * ROWS, HEAD), BF), blocks(4, F32),
        blocks(2, F32), one(jnp.int32),
        tall(ROWS, BF), pltpu.VMEM((ROWS, 2 * ROWS), F32), tall(ROWS, F32), full(BF),
        stats, blocks(NY, BF), one(F32), one(F32), one(F32), one(BF),
        pltpu.VMEM((ROWS, 2 * ROWS), BF), tall(HEAD, F32), tall(HEAD, F32),
        blocks(2, BF), blocks(2, BF),
        blocks(NY, F32), blocks(NY, BF), blocks(NY - 1, BF), stats,
        full(BF), one(BF), one(BF), tall(2 * HEAD, BF), blocks(2, F32),
        *reduce_scratch(NX, NZ, 16, BF),
        *reduce3_scratch(2 * HEAD),
        *reduce3_scratch(HEAD),
        pltpu.SemaphoreType.DMA((5,)),
        pltpu.SemaphoreType.DMA((8,)),
        pltpu.SemaphoreType.DMA((160,)),
        pltpu.SemaphoreType.DMA((160,)),
    ]
    shapes = (
        jax.ShapeDtypeStruct((ROWS, HEAD), BF),
        jax.ShapeDtypeStruct((ROWS, HEAD), BF),
        jax.ShapeDtypeStruct((WIDTH, 4 * HEAD), F32),
        jax.ShapeDtypeStruct((HEAD, WIDTH), F32),
    )
    results = pl.pallas_call(
        kernel,
        out_shape=shapes,
        in_specs=[hbm] * 5,
        out_specs=(hbm,) * 4,
        scratch_shapes=scratch,
        compiler_params=pltpu.CompilerParams(
            collective_id=0, has_side_effects=True, vmem_limit_bytes=62 * 1024 * 1024
        ),
        name="layer",
    )(tokens, lengths, weight_in, weight_out, grad_out)
    return pl.pallas_call(
        store,
        out_shape=shapes,
        in_specs=[hbm] * 4,
        out_specs=(hbm,) * 4,
        scratch_shapes=[pltpu.VMEM(shape.shape, shape.dtype) for shape in shapes]
        + [pltpu.SemaphoreType.DMA((7,))] * 2,
        name="store",
    )(*results)


def solution(mesh):
    placed = (P("dp", "sub"), P(), P(None, "sub"), P("sub", None), P("dp", "sub"))
    return jax.shard_map(
        shards,
        mesh=mesh,
        in_specs=placed,
        out_specs=(P("dp", "sub"), P("dp", "sub"), P(None, "sub"), P("sub", None)),
        check_vma=False,
    )
```

time: 61.1 us -> 59.1 us (0.967)
  Pallas kernels: 60.3 us -> 58.3 us
    pallas_call x2, Pallas kernels: 60.3 us -> 58.3 us  [the longest x1 56 us: shards(): pl.pallas_call(kernel, out_shape=shapes, in_specs=[hbm] * 5, out_specs=(h...]
where the time goes in v3:
time: 59.1 us; the launch traced here: 58.9 us
  Pallas kernels  58.3 us (99%)
  between operations  0.64 us (1%)
    pallas_call x1, Pallas kernels, shards(): pl.pallas_call(kernel, out_shape=shapes, in_specs=[hbm] * 5, out_specs=(h...  56 us
    pallas_call x1, Pallas kernels, shards(): pl.pallas_call(store, out_shape=shapes, in_specs=[hbm] * 4, out_specs=(hb...  2.25 us

profile of v3, /device:TPU:1, one launch (start us, length us, event | category | flops | bytes accessed | tf_op | source)
XLA Modules:
  0.0 58.9 jit_solution(8957330977748828454)
XLA Ops:
  0.6 56.0 %layer.1 = (bf16[512,128]{1,0:T(8,128)(2,1)}, bf16[512,128]{1,0:T(8,128)(2,1)}, f32[512,512]{1,0:T(8,128)}, f32[128,512]{1,0:T(8,128)}) custom-call(bf16[512,128]{1,0:T(8,128)(2,1)} %tok_h.1, s32[1,128]{1,0:T(1,128)} %bitcast.1, bf16[512,512]{1,0:T(8,128)(2,1)} %win_h.1, bf16[128,512]{1,0:T(8,128)(2,1)} %wout_h.1, bf16[512,128]{1,0:T(8,128)(2,1)} %gout_h.1), custom_call_target="tpu_custom_call" | custom-call | tf_op jit(solution)/shard_map/layer/pallas_call | solution.py:620
  56.7 2.3 %store.1 = (bf16[512,128]{1,0:T(8,128)(2,1)}, bf16[512,128]{1,0:T(8,128)(2,1)}, f32[512,512]{1,0:T(8,128)}, f32[128,512]{1,0:T(8,128)}) custom-call(bf16[512,128]{1,0:T(8,128)(2,1)} %get-tuple-element.8.refs_0_, bf16[512,128]{1,0:T(8,128)(2,1)} %get-tuple-element.9.refs_1_, f32[512,512]{1,0:T(8,128)} %get-tuple-element.10.refs_2_, ...), custom_call_target="tpu_custom_call" | custom-call | tf_op jit(solution)/shard_map/store/pallas_call | solution.py:631

commit v4 on v3

--- a/solution.py
+++ b/solution.py
@@ -24,30 +24,31 @@
     return lax.dot_general(left, right, dims, preferred_element_type=F32)
 
 
-class Copy:
-    def __init__(self, copy):
-        self.copy, self.left, self.landed = copy, False, False
-        copy.start()
+class Exchange:
+    def __init__(self, make, whole):
+        self.make, self.whole = make, whole
+
+    def add(self, src, dst, device):
+        self.make(src, dst, device).start()
+        self.device = device
+        return self
 
     def wait_recv(self):
-        if not self.landed:
-            self.copy.wait_recv()
-        self.landed = True
+        self.make(self.whole, self.whole, self.device).wait_recv()
 
     def wait_send(self):
-        if not self.left:
-            self.copy.wait_send()
-        self.left = True
+        self.make(self.whole, self.whole, self.device).wait_send()
 
 
 class Sender:
     def __init__(self, send_sem, recv_sem):
-        self.send_sem, self.recv_sem, self.copies = send_sem, recv_sem, []
-
-    def __call__(self, src, dst, device):
-        i = len(self.copies)
-        copy = Copy(
-            pltpu.make_async_remote_copy(
+        self.send_sem, self.recv_sem, self.groups = send_sem, recv_sem, []
+
+    def group(self, whole, copies=()):
+        i = len(self.groups)
+
+        def make(src, dst, device):
+            return pltpu.make_async_remote_copy(
                 src_ref=src,
                 dst_ref=dst,
                 send_sem=self.send_sem.at[i],
@@ -55,9 +56,15 @@
                 device_id=device,
                 device_id_type=MESH,
             )
-        )
-        self.copies.append(copy)
-        return copy
+
+        group = Exchange(make, whole)
+        self.groups.append(group)
+        for src, dst, device in copies:
+            group.add(src, dst, device)
+        return group
+
+    def __call__(self, src, dst, device):
+        return self.group(src, [(src, dst, device)])
 
 
 def far_first(n):
@@ -91,54 +98,50 @@
         total = self.part[...] + self.rc[...].astype(F32)
         self.part[...] = total
         self.s_1[...] = total.astype(self.dt)
-        self.w2 = []
+        self.w2 = self.send.group(self.r_1)
         for r in far_first(self.n1):
             to = self.to1(r)
-            self.w2.append(self.send(self.s_1.at[to], self.r_1.at[r - 1], self.at1(to)))
+            self.w2.add(self.s_1.at[to], self.r_1.at[r - 1], self.at1(to))
 
     def s3(self):
-        for w in self.w2:
-            w.wait_recv()
+        self.w2.wait_recv()
         total = self.part[self.i1]
         for r in range(self.n1 - 1):
             total = total + self.r_1[r].astype(F32)
         self.part[0] = total
         self.s_2[...] = total.astype(self.dt)
-        self.w3 = []
+        self.w3 = self.send.group(self.r_2)
         for r in far_first(self.n2):
             to = self.to2(r)
-            self.w3.append(self.send(self.s_2.at[to], self.r_2.at[r - 1], self.at2(to)))
+            self.w3.add(self.s_2.at[to], self.r_2.at[r - 1], self.at2(to))
 
     def s4(self):
-        for w in self.w3:
-            w.wait_recv()
+        self.w3.wait_recv()
         total = self.part[0, self.i2]
         for r in range(self.n2 - 1):
             total = total + self.r_2[r].astype(F32)
         mine = self.full.at[self.c, self.i1, self.i2]
         self.full[self.c, self.i1, self.i2] = (total * self.scale).astype(self.dt)
-        self.w4 = [
-            self.send(mine, mine, self.at2(self.to2(r))) for r in far_first(self.n2)
-        ]
+        self.w4 = self.send.group(
+            self.r_2, [(mine, mine, self.at2(self.to2(r))) for r in far_first(self.n2)]
+        )
 
     def s5(self):
-        for w in self.w4:
-            w.wait_recv()
+        self.w4.wait_recv()
         mine = self.full.at[self.c, self.i1]
         self.w5 = [
             (r, self.send(mine, mine, self.at1(self.to1(r)))) for r in far_first(self.n1)
         ]
-        self.w6 = [self.send(mine, mine, self.core)]
+        self.w6 = self.send.group(self.s_1, [(mine, mine, self.core)])
 
     def s6(self):
         for r, w in self.w5[::-1]:
             w.wait_recv()
             piece = self.full.at[self.c, lax.rem(self.i1 + self.n1 - r, self.n1)]
-            self.w6.append(self.send(piece, piece, self.core))
+            self.w6.add(piece, piece, self.core)
 
     def s7(self):
-        for w in self.w6:
-            w.wait_recv()
+        self.w6.wait_recv()
 
 
 class Reduce3:
@@ -162,47 +165,50 @@
         total = self.part[...] + self.rc[...].astype(F32)
         self.part[...] = total
         self.s_1[...] = total.astype(self.dt)
-        self.w2 = []
+        self.w2 = self.send.group(self.r_1)
         for r in far_first(self.n1):
             to = lax.rem(self.i1 + r, self.n1)
-            self.w2.append(self.send(self.s_1.at[to], self.r_1.at[r - 1], self.at1(to)))
+            self.w2.add(self.s_1.at[to], self.r_1.at[r - 1], self.at1(to))
 
     def s3(self):
-        for w in self.w2:
-            w.wait_recv()
+        self.w2.wait_recv()
         total = self.part[self.i1]
         for r in range(self.n1 - 1):
             total = total + self.r_1[r].astype(F32)
         self.both[self.i2] = total.astype(self.dt)
         mine = self.both.at[self.i2]
-        self.w3 = [
-            self.send(mine, mine, self.at2(lax.rem(self.i2 + r, self.n2)))
-            for r in far_first(self.n2)
-        ]
+        self.w3 = self.send.group(
+            self.both.at[0 : self.n2 - 1],
+            [
+                (mine, mine, self.at2(lax.rem(self.i2 + r, self.n2)))
+                for r in far_first(self.n2)
+            ],
+        )
 
     def s4(self):
-        for w in self.w3:
-            w.wait_recv()
+        self.w3.wait_recv()
         total = self.both[0].astype(F32)
         for k in range(1, self.n2):
             total = total + self.both[k].astype(F32)
         self.full[self.c, self.i1] = (total * self.scale).astype(self.dt)
         mine = self.full.at[self.c, self.i1]
-        self.w4 = [
-            (r, self.send(mine, mine, self.at1(lax.rem(self.i1 + r, self.n1))))
-            for r in far_first(self.n1)
-        ]
-        self.w5 = [self.send(mine, mine, self.core)]
+        order = far_first(self.n1)
+        self.w4 = []
+        for steps in (order[:3], order[3:]):
+            peers = [self.at1(lax.rem(self.i1 + r, self.n1)) for r in steps]
+            whole = self.r_1.at[0 : len(steps)]
+            self.w4.append((steps, self.send.group(whole, [(mine, mine, to) for to in peers])))
+        self.w5 = self.send.group(self.s_1, [(mine, mine, self.core)])
 
     def s5(self):
-        for r, w in self.w4[::-1]:
+        for steps, w in self.w4[::-1]:
             w.wait_recv()
-            piece = self.full.at[self.c, lax.rem(self.i1 + self.n1 - r, self.n1)]
-            self.w5.append(self.send(piece, piece, self.core))
+            for r in steps:
+                piece = self.full.at[self.c, lax.rem(self.i1 + self.n1 - r, self.n1)]
+                self.w5.add(piece, piece, self.core)
 
     def s6(self):
-        for w in self.w5:
-            w.wait_recv()
+        self.w5.wait_recv()
 
 
 def column(value):
@@ -222,8 +228,8 @@
 
 def kernel(
     tok_h, len_h, win_h, wout_h, gout_h,
-    lo, gt, gwin, gwout,
-    lens, win, wout, lo_v, gt_v, gwin_v, gwout_v,
+    lo, gt, g_vk, g_q, g_uo,
+    lens, win, wout, lo_v, gt_v,
     xg, gg, wc, xh, xn, xnt, xnp, xr, gate, qb, kv, slope, slope_p, srow,
     wt, sl, slt, wp,
     stat, gat, att, ee, dgate, datt, ds, dk, dv, dkv_s, dkv_r,
@@ -287,15 +293,21 @@
     half = ROWS // 2
     low, high = slice(0, half), slice(half, ROWS)
 
-    got_x = []
-    for rows in tiles:
-        got_x.append([send(xg.at[y, rows], xg.at[y, rows], (d, peer)) for _, peer in y_peers])
+    def gather(own, whole):
+        return send.group(whole, [(own, own, (d, peer)) for _, peer in y_peers])
+
+    got_x = [gather(xg.at[y, rows], xg.at[0 : NY - 1, rows]) for rows in tiles[:-1]]
     pass_up = send(gg.at[y, low], gg.at[y, low], (d, y_up))
     pass_down = send(gg.at[y, high], gg.at[y, high], (d, y_down))
-    got_g = [
-        send(gg.at[y, high], gg.at[y, high], (d, y_up)),
-        send(gg.at[y, low], gg.at[y, low], (d, y_down)),
-    ]
+    rows = tiles[-1]
+    got_x.append(gather(xg.at[y, rows], xg.at[0 : NY - 1, rows]))
+    got_g = send.group(
+        gg.at[0:2],
+        [
+            (gg.at[y, high], gg.at[y, high], (d, y_up)),
+            (gg.at[y, low], gg.at[y, low], (d, y_down)),
+        ],
+    )
     srow[...] = jnp.broadcast_to(
         start_rows(lens, d * ROWS).astype(jnp.int32), (ROWS, 128)
     )
@@ -316,8 +328,14 @@
 
     got_kv = []
     for t, rows in enumerate(tiles):
-        for w in got_x[t]:
-            w.wait_recv()
+        if t == len(tiles) - 1:
+            pass_up.wait_recv()
+            slot = gg.at[y_down, low]
+            got_g.add(slot, slot, (d, y_up))
+            pass_down.wait_recv()
+            slot = gg.at[y_up, high]
+            got_g.add(slot, slot, (d, y_down))
+        got_x[t].wait_recv()
         parts = [xg[b, rows].astype(F32) for b in range(NY)]
         mean = column(parts[0] + parts[1] + parts[2] + parts[3]) * (1.0 / WIDTH)
         parts = [part - mean for part in parts]
@@ -341,13 +359,6 @@
         for i, g in enumerate((0, 2, 1, 3)):
             slope[i, rows] = slopes[:, g * HEAD : (g + 1) * HEAD]
 
-    pass_up.wait_recv()
-    slot = gg.at[y_down, low]
-    got_g.append(send(slot, slot, (d, y_up)))
-    pass_down.wait_recv()
-    slot = gg.at[y_up, high]
-    got_g.append(send(slot, slot, (d, y_down)))
-
     for t, rows in enumerate(tiles):
         weight, tangent = attend(
             mm(qb[rows, :], kv[1, ROWS:], NT), srow[rows, 0:1], 0, t * TILE
@@ -368,8 +379,7 @@
         sl[:, cols] = tangent
         att[...] = att[...] + mm(weight, kv[0, cols])
 
-    for w in got_g:
-        w.wait_recv()
+    got_g.wait_recv()
     d_gated = sum(
         mm(gg[b], wout[:, b * HEAD : (b + 1) * HEAD], NT) for b in range(NY)
     )
@@ -387,12 +397,11 @@
                   jnp.where(lane == 2, column(e), jnp.where(lane == 3, column(e * ca), 0.0))),
     )
     stat[y] = packed.T[:8]
-    got_s = [send(stat.at[y], stat.at[y], (d, peer)) for _, peer in y_peers]
+    got_s = gather(stat.at[y], stat.at[0 : NY - 1])
     for rows in tiles:
         wt[rows, :] = wp[:, rows].T
         slt[rows, :] = sl[:, rows].T
-    for w in got_s:
-        w.wait_recv()
+    got_s.wait_recv()
     heads = [stat[h] for h in range(NY)]
     mean = sum(h[0:1] for h in heads) * (1.0 / WIDTH)
     var, s_e, s_en = 0.0, 0.0, 0.0
@@ -413,15 +422,18 @@
     normed = (att[...] - mean) * inv
     datt[...] = (inv * (ee[...] - s_e - normed * s_en)).astype(BF)
     gat[y] = (normed * gate[...].astype(F32)).astype(BF)
-    got_a = [send(gat.at[y], gat.at[y], (d, peer)) for _, peer in y_peers]
-    got_w = [
-        send(
-            wout.at[:, pl.ds(pl.multiple_of(peer * HEAD, HEAD), HEAD)],
-            wc.at[y],
-            (d, peer),
-        )
-        for _, peer in y_peers
-    ]
+    got_a = gather(gat.at[y], gat.at[0 : NY - 1])
+    got_w = send.group(
+        wc.at[0 : NY - 1],
+        [
+            (
+                wout.at[:, pl.ds(pl.multiple_of(peer * HEAD, HEAD), HEAD)],
+                wc.at[y],
+                (d, peer),
+            )
+            for _, peer in y_peers
+        ],
+    )
     dh_u[...] = (dgate[...] * normed * slope[0]).astype(BF)
 
     gated_t = gat[y].T
@@ -485,10 +497,13 @@
         din_s[b] = part.astype(BF)
     packed = jnp.where(lane == 0, column(one), jnp.where(lane == 1, column(two), 0.0))
     stat2[y] = packed.T[:8]
-    got_i = [send(din_s.at[peer], din_r.at[r - 1], (d, peer)) for r, peer in y_peers]
-    got_t = [send(stat2.at[y], stat2.at[y], (d, peer)) for _, peer in y_peers]
-    for w in got_a + got_w:
-        w.wait_recv()
+    got_i = send.group(
+        din_r, [(din_s.at[peer], din_r.at[r - 1], (d, peer)) for r, peer in y_peers]
+    )
+    got_t = gather(stat2.at[y], stat2.at[0 : NY - 1])
+
+    got_a.wait_recv()
+    got_w.wait_recv()
     lo_v[...] = (
         xg[y].astype(F32) + sum(mm(gat[h], wc[h]) for h in range(NY))
     ).astype(BF)
@@ -500,8 +515,8 @@
     r_q.s4()
     r_uo.s5()
 
-    for w in got_i + got_t:
-        w.wait_recv()
+    got_i.wait_recv()
+    got_t.wait_recv()
     total = din[y]
     for r in range(NY - 1):
         total = total + din_r[r].astype(F32)
@@ -511,47 +526,58 @@
     gt_v[...] = (gg[y].astype(F32) + piece).astype(BF)
     put(gt_v, gt)
 
-    def put_columns(g, value):
-        cols = slice(g * HEAD, (g + 1) * HEAD)
-        gwin_v[:, cols] = value.astype(F32)
-        put(gwin_v.at[:, cols], gwin.at[:, cols])
-
     r_vk.s5()
     r_q.s5()
     r_uo.s6()
     r_vk.s6()
-    done = r_vk.full[...].reshape(ROWS, 2 * HEAD)
-    put_columns(1, done[:, :HEAD])
-    put_columns(3, done[:, HEAD:])
+    put(r_vk.full, g_vk)
     r_q.s6()
-    put_columns(2, r_q.full[...].reshape(ROWS, HEAD))
+    put(r_q.full, g_q)
     r_uo.s7()
-    put_columns(0, r_uo.full[0].reshape(ROWS, HEAD))
-    for b in range(NY):
-        gwout_v[:, b * HEAD : (b + 1) * HEAD] = r_uo.full[1, b].reshape(HEAD, HEAD).astype(F32)
-    put(gwout_v, gwout)
-    for w in send.copies:
+    put(r_uo.full, g_uo)
+    for w in send.groups:
         w.wait_send()
     for w in stores:
         w.wait()
 
 
-def store(*refs):
-    sources, targets, stages, sems = refs[:4], refs[4:8], refs[8:12], refs[12:]
-    parts = [(i, slice(None)) for i in (0, 1, 3)]
-    parts += [(2, slice(t * TILE, (t + 1) * TILE)) for t in range(WIDTH // TILE)]
-    reads, writes = [], []
-    for n, (i, rows) in enumerate(parts):
-        stage = stages[i].at[rows]
-        reads.append(pltpu.make_async_copy(sources[i].at[rows], stage, sems[0].at[n]))
-        writes.append(pltpu.make_async_copy(stage, targets[i].at[rows], sems[1].at[n]))
-    for read in reads:
-        read.start()
-    for read, write in zip(reads, writes):
-        read.wait()
-        write.start()
-    for write in writes:
-        write.wait()
+def store(
+    lo_h, gt_h, vk_h, q_h, uo_h, lo, gt, gwin, gwout,
+    lo_v, gt_v, vk, q, uo, gwin_v, gwout_v, read_sem, write_sem,
+):
+    pairs = [(lo_h, lo_v), (gt_h, gt_v), (vk_h, vk), (q_h, q), (uo_h, uo)]
+    reads = [
+        pltpu.make_async_copy(src, dst, read_sem.at[i]) for i, (src, dst) in enumerate(pairs)
+    ]
+    writes = []
+
+    def write(src, dst):
+        writes.append(pltpu.make_async_copy(src, dst, write_sem.at[len(writes)]))
+        writes[-1].start()
+
+    def write_columns(g, value):
+        cols = slice(g * HEAD, (g + 1) * HEAD)
+        gwin_v[:, cols] = value.reshape(ROWS, HEAD).astype(F32)
+        write(gwin_v.at[:, cols], gwin.at[:, cols])
+
+    for i in (2, 3, 4, 0, 1):
+        reads[i].start()
+    reads[2].wait()
+    write_columns(1, vk[:, :, :, :HEAD])
+    write_columns(3, vk[:, :, :, HEAD:])
+    reads[3].wait()
+    write_columns(2, q[...])
+    reads[4].wait()
+    write_columns(0, uo[0])
+    for b in range(NY):
+        gwout_v[:, b * HEAD : (b + 1) * HEAD] = uo[1, b].reshape(HEAD, HEAD).astype(F32)
+    write(gwout_v, gwout)
+    reads[0].wait()
+    write(lo_v, lo)
+    reads[1].wait()
+    write(gt_v, gt)
+    for copy in writes:
+        copy.wait()
 
 
 def reduce3_scratch(n):
@@ -592,7 +618,7 @@
     stats = pltpu.VMEM((NY, 8, ROWS), F32)
     scratch = [
         pltpu.VMEM((1, 128), jnp.int32), full(BF), pltpu.VMEM((HEAD, WIDTH), BF),
-        one(BF), one(BF), full(F32), pltpu.VMEM((HEAD, WIDTH), F32),
+        one(BF), one(BF),
         blocks(NY, BF), blocks(NY, BF), pltpu.VMEM((NY, HEAD, HEAD), BF),
         blocks(NY, F32), full(BF), pltpu.VMEM((WIDTH, 2 * ROWS), BF), full(BF), one(F32),
         one(BF), one(BF), pltpu.VMEM((2, 2 * ROWS, HEAD), BF), blocks(4, F32),
@@ -607,10 +633,17 @@
         *reduce3_scratch(2 * HEAD),
         *reduce3_scratch(HEAD),
         pltpu.SemaphoreType.DMA((5,)),
-        pltpu.SemaphoreType.DMA((8,)),
-        pltpu.SemaphoreType.DMA((160,)),
-        pltpu.SemaphoreType.DMA((160,)),
+        pltpu.SemaphoreType.DMA((5,)),
+        pltpu.SemaphoreType.DMA((39,)),
+        pltpu.SemaphoreType.DMA((39,)),
     ]
+    rounded = (
+        (ROWS, HEAD),
+        (ROWS, HEAD),
+        (NC, NZ, ROWS // (NC * NZ), 2 * HEAD),
+        (NC, NZ, ROWS // (NC * NZ), HEAD),
+        (NC, NX, NZ, 16, HEAD),
+    )
     shapes = (
         jax.ShapeDtypeStruct((ROWS, HEAD), BF),
         jax.ShapeDtypeStruct((ROWS, HEAD), BF),
@@ -619,9 +652,9 @@
     )
     results = pl.pallas_call(
         kernel,
-        out_shape=shapes,
+        out_shape=tuple(jax.ShapeDtypeStruct(shape, BF) for shape in rounded),
         in_specs=[hbm] * 5,
-        out_specs=(hbm,) * 4,
+        out_specs=(hbm,) * 5,
         scratch_shapes=scratch,
         compiler_params=pltpu.CompilerParams(
             collective_id=0, has_side_effects=True, vmem_limit_bytes=62 * 1024 * 1024
@@ -631,10 +664,12 @@
     return pl.pallas_call(
         store,
         out_shape=shapes,
-        in_specs=[hbm] * 4,
+        in_specs=[hbm] * 5,
         out_specs=(hbm,) * 4,
-        scratch_shapes=[pltpu.VMEM(shape.shape, shape.dtype) for shape in shapes]
-        + [pltpu.SemaphoreType.DMA((7,))] * 2,
+        scratch_shapes=[pltpu.VMEM(shape, BF) for shape in rounded]
+        + [full(F32), pltpu.VMEM((HEAD, WIDTH), F32)]
+        + [pltpu.SemaphoreType.DMA((5,)), pltpu.SemaphoreType.DMA((7,))],
+        compiler_params=pltpu.CompilerParams(vmem_limit_bytes=62 * 1024 * 1024),
         name="store",
     )(*results)
 

time: 59.1 us -> 56.2 us (0.951)
  Pallas kernels: 58.3 us -> 55.4 us
    pallas_call x2, Pallas kernels: 58.3 us -> 55.4 us  [the longest x1 53.2 us: shards(): pl.pallas_call(kernel, out_shape=tuple((jax.ShapeDtypeStruct(shape, BF) f...]
where the time goes in v4:
time: 56.2 us; the launch traced here: 56 us
  Pallas kernels  55.4 us (99%)
  between operations  0.64 us (1%)
    pallas_call x1, Pallas kernels, shards(): pl.pallas_call(kernel, out_shape=tuple((jax.ShapeDtypeStruct(shape, BF) f...  53.2 us
    pallas_call x1, Pallas kernels, shards(): pl.pallas_call(store, out_shape=shapes, in_specs=[hbm] * 5, out_specs=(hb...  2.22 us

profile of v4, /device:TPU:1, one launch (start us, length us, event | category | flops | bytes accessed | tf_op | source)
XLA Modules:
  0.0 56.0 jit_solution(760253385826316714)
XLA Ops:
  0.6 53.2 %layer.1 = (bf16[512,128]{1,0:T(8,128)(2,1)}, bf16[512,128]{1,0:T(8,128)(2,1)}, bf16[2,8,32,256]{3,2,1,0:T(8,128)(2,1)}, bf16[2,8,32,128]{3,2,1,0:T(8,128)(2,1)}, bf16[2,4,8,16,128]{4,3,2,1,0:T(8,128)(2,1)}) custom-call(bf16[512,128]{1,0:T(8,128)(2,1)} %tok_h.1, s32[1,128]{1,0:T(1,128)} %bitcast.1, bf16[512,512]{1,0:T(8,128)(2,1)} %win_h.1, ...), custom_call_target="tpu_custom_call" | custom-call | tf_op jit(solution)/shard_map/layer/pallas_call | solution.py:653
  53.8 2.2 %store.1 = (bf16[512,128]{1,0:T(8,128)(2,1)}, bf16[512,128]{1,0:T(8,128)(2,1)}, f32[512,512]{1,0:T(8,128)}, f32[128,512]{1,0:T(8,128)}) custom-call(bf16[512,128]{1,0:T(8,128)(2,1)} %get-tuple-element.9.lo_h, bf16[512,128]{1,0:T(8,128)(2,1)} %get-tuple-element.10.gt_h, bf16[2,8,32,256]{3,2,1,0:T(8,128)(2,1)} %get-tuple-element.11.vk_h, ...), custom_call_target="tpu_custom_call" | custom-call | tf_op jit(solution)/shard_map/store/pallas_call | solution.py:664

commit v5 on v4

--- a/solution.py
+++ b/solution.py
@@ -233,7 +233,7 @@
     xg, gg, wc, xh, xn, xnt, xnp, xr, gate, qb, kv, slope, slope_p, srow,
     wt, sl, slt, wp,
     stat, gat, att, ee, dgate, datt, ds, dk, dv, dkv_s, dkv_r,
-    din, din_s, din_r, stat2, dhid, dh_u, dh_q, dh_vk, pair,
+    din, din_s, din_r, stat2, dhid, dh_u, dh_q, dh_vk, left, right,
     *rest,
 ):
     reduce_refs, (load_sem, out_sem, send_sem, recv_sem) = rest[:-4], rest[-4:]
@@ -270,11 +270,11 @@
         stores.append(copy)
 
     barrier = pltpu.get_barrier_semaphore()
-    greet = [(d, peer) for _, peer in y_peers]
-    greet += [at(lax.rem(x + r, NX), z, c) for r in range(1, NX)]
-    greet += [at(x, lax.rem(z + r, NZ), c) for r in range(1, NZ)]
+    greet = [at(x, lax.rem(z + r, NZ), c) for r in far_first(NZ)]
+    greet += [at(lax.rem(x + r, NX), z, c) for r in far_first(NX)]
+    greet += [(d, peer) for _, peer in y_peers]
+    greet += [(lax.rem(d + ndp + 2 * c - 1, ndp), y)]
     greet += [at(x, z, 1 - c)]
-    greet += [(lax.rem(d + ndp + 2 * c - 1, ndp), y)]
     for device in greet:
         pl.semaphore_signal(barrier, inc=1, device_id=device, device_id_type=MESH)
     for load in loads:
@@ -401,6 +401,18 @@
     for rows in tiles:
         wt[rows, :] = wp[:, rows].T
         slt[rows, :] = sl[:, rows].T
+    def block_before(t, rows):
+        got_xn[t].wait_recv()
+        for i, g in enumerate((1, 3)):
+            hidden = mm(xnp[rows, :], win[:, g * HEAD : (g + 1) * HEAD])
+            sig = 0.5 * jnp.tanh(0.5 * hidden) + 0.5
+            slope_p[i, rows] = sig * (1.0 + hidden * (1.0 - sig))
+        xnt[:, rows] = xnp[rows, :].T
+
+    for b in range(NY):
+        left[1, b * HEAD : (b + 1) * HEAD] = gg[b].T
+    left[0] = xnt[:, ROWS:]
+    block_before(0, low)
     got_s.wait_recv()
     heads = [stat[h] for h in range(NY)]
     mean = sum(h[0:1] for h in heads) * (1.0 / WIDTH)
@@ -436,34 +448,26 @@
     )
     dh_u[...] = (dgate[...] * normed * slope[0]).astype(BF)
 
-    gated_t = gat[y].T
-    pair[0] = mm(xnt[:, ROWS:], dh_u[...])
-    for b in range(NY):
-        pair[1, b * HEAD : (b + 1) * HEAD] = mm(gated_t, gg[b])
-    r_uo.s1(pair[1 - c])
-    r_uo.keep(pair[c])
-
-    def key_grads(rows):
-        d_st = (mm(kv[0, rows], datt[...], NT) * slt[rows, :]).astype(BF)
-        dk[rows, :] = mm(d_st, qb[...])
-        dv[rows, :] = mm(wt[rows, :], datt[...])
+    right[0] = dh_u[...]
+    right[1] = gat[y]
+    r_uo.s1(mm(left[1 - c], right[1 - c]))
+
+    def key_grads(rows, first):
+        d_st = (mm(kv[0, rows], datt[first:, :], NT) * slt[rows, first:]).astype(BF)
+        dk[rows, :] = mm(d_st, qb[first:, :])
+        dv[rows, :] = mm(wt[rows, first:], datt[first:, :])
 
     for t in range(ROWS // TILE):
-        key_grads(tiles[t])
+        key_grads(tiles[t], 0)
     dkv_s[0] = dv[:ROWS, :].astype(BF)
     dkv_s[1] = dk[:ROWS, :].astype(BF)
     got_dkv = send(dkv_s, dkv_r, below)
+    r_uo.keep(mm(left[c], right[c]))
+    r_uo.s2()
     for t in range(ROWS // TILE):
-        key_grads(slice(ROWS + t * TILE, ROWS + (t + 1) * TILE))
-    r_uo.s2()
-
-    for t, rows in enumerate((low, high)):
-        got_xn[t].wait_recv()
-        for i, g in enumerate((1, 3)):
-            hidden = mm(xnp[rows, :], win[:, g * HEAD : (g + 1) * HEAD])
-            sig = 0.5 * jnp.tanh(0.5 * hidden) + 0.5
-            slope_p[i, rows] = sig * (1.0 + hidden * (1.0 - sig))
-        xnt[:, rows] = xnp[rows, :].T
+        key_grads(slice(ROWS + t * TILE, ROWS + (t + 1) * TILE), t * TILE)
+
+    block_before(1, high)
     dh_vk[:ROWS, :HEAD] = (dv[:ROWS, :] * slope_p[0]).astype(BF)
     dh_vk[:ROWS, HEAD:] = (dk[:ROWS, :] * slope_p[1]).astype(BF)
     dh_vk[ROWS:, :HEAD] = (dv[ROWS:, :] * slope[2]).astype(BF)
@@ -509,8 +513,8 @@
     ).astype(BF)
     put(lo_v, lo)
     r_vk.s3()
+    r_uo.s4()
     r_q.s3()
-    r_uo.s4()
     r_vk.s4()
     r_q.s4()
     r_uo.s5()
@@ -569,8 +573,7 @@
     write_columns(2, q[...])
     reads[4].wait()
     write_columns(0, uo[0])
-    for b in range(NY):
-        gwout_v[:, b * HEAD : (b + 1) * HEAD] = uo[1, b].reshape(HEAD, HEAD).astype(F32)
+    gwout_v[...] = uo[1].reshape(WIDTH, HEAD).astype(F32).T
     write(gwout_v, gwout)
     reads[0].wait()
     write(lo_v, lo)
@@ -628,7 +631,7 @@
         pltpu.VMEM((ROWS, 2 * ROWS), BF), tall(HEAD, F32), tall(HEAD, F32),
         blocks(2, BF), blocks(2, BF),
         blocks(NY, F32), blocks(NY, BF), blocks(NY - 1, BF), stats,
-        full(BF), one(BF), one(BF), tall(2 * HEAD, BF), blocks(2, F32),
+        full(BF), one(BF), one(BF), tall(2 * HEAD, BF), pltpu.VMEM((2, WIDTH, ROWS), BF), blocks(2, BF),
         *reduce_scratch(NX, NZ, 16, BF),
         *reduce3_scratch(2 * HEAD),
         *reduce3_scratch(HEAD),

time: 56.2 us -> 55.8 us (level)
  no operation moved by 1% of the time
where the time goes in v5:
time: 55.8 us; the launch traced here: 55.7 us
  Pallas kernels  55 us (99%)
  between operations  0.64 us (1%)
    pallas_call x1, Pallas kernels, shards(): pl.pallas_call(kernel, out_shape=tuple((jax.ShapeDtypeStruct(shape, BF) f...  52.8 us
    pallas_call x1, Pallas kernels, shards(): pl.pallas_call(store, out_shape=shapes, in_specs=[hbm] * 5, out_specs=(hb...  2.22 us

profile of v5, /device:TPU:1, one launch (start us, length us, event | category | flops | bytes accessed | tf_op | source)
XLA Modules:
  0.0 55.7 jit_solution(6511270347283987971)
XLA Ops:
  0.6 52.8 %layer.1 = (bf16[512,128]{1,0:T(8,128)(2,1)}, bf16[512,128]{1,0:T(8,128)(2,1)}, bf16[2,8,32,256]{3,2,1,0:T(8,128)(2,1)}, bf16[2,8,32,128]{3,2,1,0:T(8,128)(2,1)}, bf16[2,4,8,16,128]{4,3,2,1,0:T(8,128)(2,1)}) custom-call(bf16[512,128]{1,0:T(8,128)(2,1)} %tok_h.1, s32[1,128]{1,0:T(1,128)} %bitcast.1, bf16[512,512]{1,0:T(8,128)(2,1)} %win_h.1, ...), custom_call_target="tpu_custom_call" | custom-call | tf_op jit(solution)/shard_map/layer/pallas_call | solution.py:656
  53.4 2.2 %store.1 = (bf16[512,128]{1,0:T(8,128)(2,1)}, bf16[512,128]{1,0:T(8,128)(2,1)}, f32[512,512]{1,0:T(8,128)}, f32[128,512]{1,0:T(8,128)}) custom-call(bf16[512,128]{1,0:T(8,128)(2,1)} %get-tuple-element.9.lo_h, bf16[512,128]{1,0:T(8,128)(2,1)} %get-tuple-element.10.gt_h, bf16[2,8,32,256]{3,2,1,0:T(8,128)(2,1)} %get-tuple-element.11.vk_h, ...), custom_call_target="tpu_custom_call" | custom-call | tf_op jit(solution)/shard_map/store/pallas_call | solution.py:667

commit v6 on v5

--- a/solution.py
+++ b/solution.py
@@ -564,17 +564,17 @@
         gwin_v[:, cols] = value.reshape(ROWS, HEAD).astype(F32)
         write(gwin_v.at[:, cols], gwin.at[:, cols])
 
-    for i in (2, 3, 4, 0, 1):
+    for i in (4, 2, 3, 0, 1):
         reads[i].start()
+    reads[4].wait()
+    write_columns(0, uo[0])
+    gwout_v[...] = uo[1].reshape(WIDTH, HEAD).astype(F32).T
+    write(gwout_v, gwout)
     reads[2].wait()
     write_columns(1, vk[:, :, :, :HEAD])
     write_columns(3, vk[:, :, :, HEAD:])
     reads[3].wait()
     write_columns(2, q[...])
-    reads[4].wait()
-    write_columns(0, uo[0])
-    gwout_v[...] = uo[1].reshape(WIDTH, HEAD).astype(F32).T
-    write(gwout_v, gwout)
     reads[0].wait()
     write(lo_v, lo)
     reads[1].wait()

time: 55.8 us -> 55.8 us (level)
  no operation moved by 1% of the time
where the time goes in v6:
time: 55.8 us; the launch traced here: 55.7 us
  Pallas kernels  55 us (99%)
  between operations  0.64 us (1%)
    pallas_call x1, Pallas kernels, shards(): pl.pallas_call(kernel, out_shape=tuple((jax.ShapeDtypeStruct(shape, BF) f...  52.8 us
    pallas_call x1, Pallas kernels, shards(): pl.pallas_call(store, out_shape=shapes, in_specs=[hbm] * 5, out_specs=(hb...  2.23 us

profile of v6, /device:TPU:1, one launch (start us, length us, event | category | flops | bytes accessed | tf_op | source)
XLA Modules:
  0.0 55.7 jit_solution(355491118386457028)
XLA Ops:
  0.6 52.8 %layer.1 = (bf16[512,128]{1,0:T(8,128)(2,1)}, bf16[512,128]{1,0:T(8,128)(2,1)}, bf16[2,8,32,256]{3,2,1,0:T(8,128)(2,1)}, bf16[2,8,32,128]{3,2,1,0:T(8,128)(2,1)}, bf16[2,4,8,16,128]{4,3,2,1,0:T(8,128)(2,1)}) custom-call(bf16[512,128]{1,0:T(8,128)(2,1)} %tok_h.1, s32[1,128]{1,0:T(1,128)} %bitcast.1, bf16[512,512]{1,0:T(8,128)(2,1)} %win_h.1, ...), custom_call_target="tpu_custom_call" | custom-call | tf_op jit(solution)/shard_map/layer/pallas_call | solution.py:656
  53.4 2.2 %store.1 = (bf16[512,128]{1,0:T(8,128)(2,1)}, bf16[512,128]{1,0:T(8,128)(2,1)}, f32[512,512]{1,0:T(8,128)}, f32[128,512]{1,0:T(8,128)}) custom-call(bf16[512,128]{1,0:T(8,128)(2,1)} %get-tuple-element.9.lo_h, bf16[512,128]{1,0:T(8,128)(2,1)} %get-tuple-element.10.gt_h, bf16[2,8,32,256]{3,2,1,0:T(8,128)(2,1)} %get-tuple-element.11.vk_h, ...), custom_call_target="tpu_custom_call" | custom-call | tf_op jit(solution)/shard_map/store/pallas_call | solution.py:667
